TPU v7x, 32 devices: a whole 2x2x4 slice. The times are simulated.
32 devices in a mesh: expert: 8 (over z, core), fsdp: 4 (over y, x).
Axes of the slice: x: 2, y: 2, z: 4, core: 2. Of those that a mesh axis runs over, the one named last changes fastest.
Arguments:
- states: bfloat16 [4096, 512], P(('expert', 'fsdp')), may hold values from -6 to 6
- rates: bfloat16 [4096, 512], P(('expert', 'fsdp')), may hold values from -6 to 6
- expert_ids: int32 [4096, 2], P(('expert', 'fsdp')), may hold values from 0 to 15, all different within a row; in each aligned block of 128 rows (0 to 127, 128 to 255, ...) at most 32 rows name the same one
- gate_weights: float32 [4096, 2], P(('expert', 'fsdp')), may hold values from 0.25 to 1
- cotangent: bfloat16 [4096, 512], P(('expert', 'fsdp')), may hold values from -6 to 6
- weight_in: bfloat16 [512, 16, 1024], P('fsdp', 'expert'), may hold values from -0.25 to 0.25
- weight_out: bfloat16 [1024, 16, 512], P('fsdp', 'expert'), may hold values from -0.1875 to 0.1875
Outputs:
- defect: bfloat16 [4096, 512], P(('expert', 'fsdp'))
- grad_states: bfloat16 [4096, 512], P(('expert', 'fsdp'))
- grad_in: bfloat16 [512, 16, 1024], P('fsdp', 'expert')
- grad_out: bfloat16 [1024, 16, 512], P('fsdp', 'expert')
Inputs may be any that keep to these rules, and one draw needn't show every extreme that they name: `expert_ids`: A knot's two ids differ. Within each aligned block of 128 knots (the knots of one device) no expert is named by more than 32 of the block's entries, a bound that some block reaches.
All inputs are finite; a program needn't handle non-finite values.
Results may differ from a plain program's by a relative error of at most 0.019.
Values may be sent and summed in bfloat16 or wider, within the bound.
A program may use at most 64 MiB of HBM per device.

v0:
```python
import jax
import jax.numpy as jnp
from jax import lax
from jax.sharding import PartitionSpec as P


def activate(value):
    return value * jax.nn.sigmoid(value)


def activate_slope(value):
    sigma = jax.nn.sigmoid(value)
    return sigma * (1.0 + value * (1.0 - sigma))


def on_device(states, rates, expert_ids, gate_weights, cotangent, weight_in, weight_out):
    row_count = states.shape[0]
    feature = states.shape[1]
    local_count = weight_in.shape[1]
    groups = lax.axis_size("expert")
    experts_all = local_count * groups
    capacity = max(2, 4 * row_count // experts_all)
    assigned = 2 * row_count
    flat_ids = expert_ids.reshape(assigned)
    onehot = (flat_ids[:, None] == jnp.arange(experts_all, dtype=jnp.int32)[None, :]).astype(
        jnp.int32
    )
    before = jnp.cumsum(onehot, axis=0) - onehot
    slot_index = jnp.sum(before * onehot, axis=1)
    position = flat_ids * capacity + slot_index
    source = jnp.full((experts_all * capacity,), assigned, jnp.int32)
    source = source.at[position].set(jnp.arange(assigned, dtype=jnp.int32))
    zero_row = jnp.zeros((1, feature), jnp.bfloat16)
    padded_states = jnp.concatenate([states, zero_row], axis=0)
    descent = (-gate_weights[:, :, None] * cotangent[:, None, :].astype(jnp.float32)).astype(
        jnp.bfloat16
    )
    padded_descent = jnp.concatenate([descent.reshape(assigned, feature), zero_row], axis=0)
    send_shape = (experts_all, capacity, feature)
    send_knots = padded_states[source // 2].reshape(send_shape)
    send_grads = padded_descent[source].reshape(send_shape)
    got_knots = lax.all_to_all(send_knots, "expert", split_axis=0, concat_axis=0, tiled=True)
    got_grads = lax.all_to_all(send_grads, "expert", split_axis=0, concat_axis=0, tiled=True)
    recv_shape = (groups, local_count, capacity, feature)
    knot_rows = got_knots.reshape(recv_shape)
    grad_rows = got_grads.reshape(recv_shape)
    part = knot_rows
    preact = jnp.einsum(
        "secd,deh->sech",
        part,
        lax.all_gather(weight_in, "fsdp", axis=0, tiled=True),
        preferred_element_type=jnp.float32,
    )
    hidden = activate(preact).astype(jnp.bfloat16)
    part = hidden
    values = jnp.einsum(
        "sech,hed->secd",
        part,
        lax.all_gather(weight_out, "fsdp", axis=0, tiled=True),
        preferred_element_type=jnp.float32,
    )
    slope = jnp.einsum(
        "secd,hed->sech",
        grad_rows,
        lax.all_gather(weight_out, "fsdp", axis=0, tiled=True),
        preferred_element_type=jnp.float32,
    )
    inner = (slope * activate_slope(preact)).astype(jnp.bfloat16)
    returned = jnp.einsum(
        "sech,deh->secd",
        inner,
        lax.all_gather(weight_in, "fsdp", axis=0, tiled=True),
        preferred_element_type=jnp.float32,
    )
    values_send = values.astype(jnp.bfloat16).reshape(send_shape)
    returned_send = returned.astype(jnp.bfloat16).reshape(send_shape)
    values_back = lax.all_to_all(values_send, "expert", split_axis=0, concat_axis=0, tiled=True)
    returned_back = lax.all_to_all(returned_send, "expert", split_axis=0, concat_axis=0, tiled=True)
    values_knot = values_back.reshape(experts_all * capacity, feature)[position]
    values_knot = values_knot.reshape(row_count, 2, feature).astype(jnp.float32)
    combined = jnp.sum(gate_weights[:, :, None] * values_knot, axis=1)
    defect = (rates.astype(jnp.float32) - combined).astype(jnp.bfloat16)
    returned_knot = returned_back.reshape(experts_all * capacity, feature)[position]
    returned_knot = returned_knot.reshape(row_count, 2, feature).astype(jnp.float32)
    grad_states = jnp.sum(returned_knot, axis=1).astype(jnp.bfloat16)
    part = knot_rows
    grad_in = lax.psum_scatter(
        jnp.einsum("secd,sech->deh", part, inner, preferred_element_type=jnp.float32).astype(
            jnp.bfloat16
        ),
        "fsdp",
        scatter_dimension=0,
        tiled=True,
    )
    part = hidden
    grad_out = lax.psum_scatter(
        jnp.einsum("sech,secd->hed", part, grad_rows, preferred_element_type=jnp.float32).astype(
            jnp.bfloat16
        ),
        "fsdp",
        scatter_dimension=0,
        tiled=True,
    )
    return (defect, grad_states, grad_in, grad_out)


def solution(mesh):
    placed = (
        P(("expert", "fsdp"), None),
        P(("expert", "fsdp"), None),
        P(("expert", "fsdp"), None),
        P(("expert", "fsdp"), None),
        P(("expert", "fsdp"), None),
        P("fsdp", "expert", None),
        P("fsdp", "expert", None),
    )
    return jax.shard_map(
        on_device,
        mesh=mesh,
        in_specs=placed,
        out_specs=(
            P(("expert", "fsdp"), None),
            P(("expert", "fsdp"), None),
            P("fsdp", "expert", None),
            P("fsdp", "expert", None),
        ),
        check_vma=False,
    )
```

profile of v0, /device:TPU:0, one launch (start us, length us, event | category | flops | bytes accessed | tf_op | source)
XLA Modules:
  0.0 174.7 jit_solution(17092730050728629836)
XLA Ops:
  7.2 2.0 %copy.37 = bf16[128,2,1024]{2,0,1:T(8,128)(2,1)} copy(bf16[128,2,1024]{2,1,0:T(2,128)(2,1)} %param.12) | data formatting | bytes 1048576 | tf_op args[5]
  9.3 1.9 %copy.39 = bf16[256,2,512]{2,0,1:T(8,128)(2,1)} copy(bf16[256,2,512]{2,1,0:T(2,128)(2,1)} %param.13) | data formatting | bytes 1048576 | tf_op args[6]
  12.9 1.4 scatter_custom_fusion
  14.3 2.6 %gather_fusion = bf16[512,512]{1,0:T(8,128)(2,1)} fusion(bf16[129,512]{1,0:T(8,128)(2,1)S(1)} %concatenate.6, s32[1024]{0:T(1024)S(1)} %get-tuple-element.21), kind=kCustom, calls=%fused_computation | custom fusion | bytes 1050624 | tf_op jit(solution)/shard_map/gather | solution.py:40
  16.9 6.3 %all-to-all-start = ((bf16[16,32,512]{2,1,0:T(8,128)(2,1)}), bf16[16,32,512]{2,1,0:T(8,128)(2,1)S(1)}, u32[]{:S(2)}, u32[]{:S(2)}) async-start(bf16[16,32,512]{2,1,0:T(8,128)(2,1)} %bitcast.3), calls=%async_computation | async-start | bytes 1048576 | tf_op jit(solution)/shard_map/all_to_all | solution.py:42
  24.2 2.6 %gather_fusion.2 = bf16[512,512]{1,0:T(8,128)(2,1)} fusion(bf16[257,512]{1,0:T(8,128)(2,1)S(1)} %concatenate.7, s32[1024]{0:T(1024)S(1)} %get-tuple-element.20), kind=kCustom, calls=%fused_computation.2 | custom fusion | bytes 1050624 | tf_op jit(solution)/shard_map/gather | solution.py:41
  26.8 11.8 %all-to-all-done = bf16[16,32,512]{2,1,0:T(8,128)(2,1)S(1)} async-done(((bf16[16,32,512]{2,1,0:T(8,128)(2,1)}), bf16[16,32,512]{2,1,0:T(8,128)(2,1)S(1)}, u32[]{:S(2)}, u32[]{:S(2)}) %all-to-all-start) | async-done | bytes 524320 | tf_op jit(solution)/shard_map/all_to_all | solution.py:42
  38.6 3.5 %all-to-all-start.2 = ((bf16[16,32,512]{2,1,0:T(8,128)(2,1)}), bf16[16,32,512]{2,1,0:T(8,128)(2,1)S(1)}, u32[]{:S(2)}, u32[]{:S(2)}) async-start(bf16[16,32,512]{2,1,0:T(8,128)(2,1)} %bitcast.13), calls=%async_computation.2 | async-start | bytes 1048576 | tf_op jit(solution)/shard_map/all_to_all | solution.py:43
  42.2 6.3 %all-gather.3.cloned.1.call-done = bf16[512,2,1024]{2,0,1:T(8,128)(2,1)} async-done(((bf16[128,2,1024]{2,0,1:T(8,128)(2,1)}), bf16[512,2,1024]{2,0,1:T(8,128)(2,1)}) %all-gather.3.cloned.1.call-update) | async-done | bytes 2097168 | tf_op jit(solution)/shard_map/all_gather | solution.py:51
  48.5 3.6 %fusion.12 = (bf16[8,2,32,1024]{3,2,0,1:T(8,128)(2,1)S(1)}, f32[2,8,32,1024]{3,2,1,0:T(8,128)}) fusion(bf16[512,2,1024]{2,0,1:T(8,128)(2,1)} %all-gather.3.cloned.1.call-done, bf16[8,2,32,512]{3,2,1,0:T(8,128)(2,1)S(1)} %bitcast.108), kind=kOutput, calls=%fused_computation.23 | convolution fusion | flops 539492352 | bytes 5767168 | tf_op jit(solution)/shard_map/secd,deh->sech/dot_general | solution.py:48
  52.1 5.3 %all-to-all-done.2 = bf16[16,32,512]{2,1,0:T(8,128)(2,1)S(1)} async-done(((bf16[16,32,512]{2,1,0:T(8,128)(2,1)}), bf16[16,32,512]{2,1,0:T(8,128)(2,1)S(1)}, u32[]{:S(2)}, u32[]{:S(2)}) %all-to-all-start.2) | async-done | bytes 524320 | tf_op jit(solution)/shard_map/all_to_all | solution.py:43
  57.4 28.3 %all-gather.5.cloned.1.call-done = bf16[1024,2,512]{2,0,1:T(8,128)(2,1)} async-done(((bf16[256,2,512]{2,0,1:T(8,128)(2,1)}), bf16[1024,2,512]{2,0,1:T(8,128)(2,1)}) %all-gather.5.cloned.1.call-update) | async-done | bytes 2097168 | tf_op jit(solution)/shard_map/all_gather | solution.py:59
  85.7 3.3 %fusion.4 = bf16[8,2,32,1024]{3,2,0,1:T(8,128)(2,1)S(1)} fusion(f32[2,8,32,1024]{3,2,1,0:T(8,128)} %get-tuple-element.19, bf16[1024,2,512]{2,0,1:T(8,128)(2,1)} %all-gather.5.cloned.1.call-done, bf16[8,2,32,512]{3,2,1,0:T(8,128)(2,1)S(1)} %bitcast.110), kind=kOutput, calls=%fused_computation.12 | convolution fusion | flops 541589504 | bytes 5767168 | tf_op jit(solution)/shard_map/secd,hed->sech/dot_general | solution.py:62
  89.9 2.5 %copy.53 = bf16[512,2048]{1,0:T(8,128)(2,1)} copy(bf16[512,2048]{0,1:T(8,128)(2,1)S(1)} %bitcast.106) | data formatting | bytes 4194304
  93.5 2.1 %fusion.15 = bf16[1024,2,512]{0,2,1:T(8,128)(2,1)} fusion(bf16[8,2,32,512]{3,2,1,0:T(8,128)(2,1)S(1)} %bitcast.111, bf16[8,2,32,1024]{3,2,0,1:T(8,128)(2,1)S(1)} %get-tuple-element.18), kind=kOutput, calls=%fused_computation.26 | convolution fusion | flops 537919488 | bytes 3670016 | tf_op jit(solution)/shard_map/sech,secd->hed/dot_general | solution.py:97
  95.6 2.8 %fusion.27 = bf16[8,2,32,512]{3,2,0,1:T(8,128)(2,1)S(1)} fusion(bf16[8,2,32,1024]{3,2,0,1:T(8,128)(2,1)} %copy-done.1, bf16[1024,2,512]{2,0,1:T(8,128)(2,1)} %all-gather.5.cloned.1.call-done), kind=kOutput, calls=%fused_computation.30 | convolution fusion | flops 537133056 | bytes 3670016 | tf_op jit(solution)/shard_map/sech,hed->secd/dot_general | solution.py:56
  99.2 4.6 %all-to-all-start.1 = ((bf16[16,32,512]{2,1,0:T(8,128)(2,1)}), bf16[16,32,512]{2,1,0:T(8,128)(2,1)S(1)}, u32[]{:S(2)}, u32[]{:S(2)}) async-start(bf16[16,32,512]{2,1,0:T(8,128)(2,1)} %bitcast.11), calls=%async_computation.1 | async-start | bytes 1048576 | tf_op jit(solution)/shard_map/all_to_all | solution.py:77
  103.8 2.0 %fusion.24 = bf16[8,2,32,512]{3,2,0,1:T(8,128)(2,1)S(1)} fusion(bf16[8,2,32,1024]{3,2,0,1:T(8,128)(2,1)} %copy-done.2, bf16[512,2,1024]{2,0,1:T(8,128)(2,1)S(1)} %copy-done), kind=kOutput, calls=%fused_computation.29 | convolution fusion | flops 537133056 | bytes 3670016 | tf_op jit(solution)/shard_map/sech,deh->secd/dot_general | solution.py:69
  106.7 12.5 %all-to-all-done.1 = bf16[16,32,512]{2,1,0:T(8,128)(2,1)S(1)} async-done(((bf16[16,32,512]{2,1,0:T(8,128)(2,1)}), bf16[16,32,512]{2,1,0:T(8,128)(2,1)S(1)}, u32[]{:S(2)}, u32[]{:S(2)}) %all-to-all-start.1) | async-done | bytes 524320 | tf_op jit(solution)/shard_map/all_to_all | solution.py:77
  119.2 3.7 %all-to-all-start.3 = ((bf16[16,32,512]{2,1,0:T(8,128)(2,1)}), bf16[16,32,512]{2,1,0:T(8,128)(2,1)S(1)}, u32[]{:S(2)}, u32[]{:S(2)}) async-start(bf16[16,32,512]{2,1,0:T(8,128)(2,1)} %bitcast.19), calls=%async_computation.3 | async-start | bytes 1048576 | tf_op jit(solution)/shard_map/all_to_all | solution.py:78
  124.1 13.8 %all-to-all-done.3 = bf16[16,32,512]{2,1,0:T(8,128)(2,1)S(1)} async-done(((bf16[16,32,512]{2,1,0:T(8,128)(2,1)}), bf16[16,32,512]{2,1,0:T(8,128)(2,1)S(1)}, u32[]{:S(2)}, u32[]{:S(2)}) %all-to-all-start.3) | async-done | bytes 524320 | tf_op jit(solution)/shard_map/all_to_all | solution.py:78
  139.2 1.3 reduce_sum.35
  144.7 21.4 %reduce-scatter.5.cloned.1.call-done = bf16[256,2,512]{0,2,1:T(8,128)(2,1)} async-done(((bf16[1024,2,512]{0,2,1:T(8,128)(2,1)}), bf16[256,2,512]{0,2,1:T(8,128)(2,1)}) %reduce-scatter.5.cloned.1.call-update) | async-done | bytes 524304 | tf_op jit(solution)/shard_map/reduce_scatter | solution.py:96
  166.1 2.0 %copy.47 = bf16[256,2,512]{2,1,0:T(2,128)(2,1)} copy(bf16[256,2,512]{0,2,1:T(8,128)(2,1)} %reduce-scatter.5.cloned.1.call-done) | data formatting | bytes 1048576
  (70 shorter events, 13.0 us)
Async XLA Ops:
  7.2 4.1 %copy-start.10 = (s32[128,2]{0,1:T(2,128)S(1)}, s32[128,2]{0,1:T(2,128)}, u32[]{:S(2)}) copy-start(s32[128,2]{0,1:T(2,128)} %param.9) | copy-start | bytes 3076
  7.2 5.6 %copy-start.8 = (bf16[128,512]{1,0:T(8,128)(2,1)S(1)}, bf16[128,512]{1,0:T(8,128)(2,1)}, u32[]{:S(2)}) copy-start(bf16[128,512]{1,0:T(8,128)(2,1)} %param.7) | copy-start | bytes 393220
  7.2 41.3 %all-gather.3.cloned.1.call-start = ((), (), s32[]{:S(2)}) async-start(), calls=%async_computation.6 | async-start | bytes 2621440 | tf_op jit(solution)/shard_map/all_gather | solution.py:51
  9.2 76.4 %all-gather.5.cloned.1.call-start = ((), (), s32[]{:S(2)}) async-start(), calls=%async_computation.7 | async-start | bytes 2621440 | tf_op jit(solution)/shard_map/all_gather | solution.py:59
  14.3 9.0 %copy-start.11 = (f32[128,2]{0,1:T(2,128)S(1)}, f32[128,2]{0,1:T(2,128)}, u32[]{:S(2)}) copy-start(f32[128,2]{0,1:T(2,128)} %param.10) | copy-start | bytes 3076
  14.3 9.2 %copy-start.7 = (bf16[128,512]{1,0:T(8,128)(2,1)S(1)}, bf16[128,512]{1,0:T(8,128)(2,1)}, u32[]{:S(2)}) copy-start(bf16[128,512]{1,0:T(8,128)(2,1)} %param.11) | copy-start | bytes 393220
  16.9 21.7 %all-to-all-start = ((bf16[16,32,512]{2,1,0:T(8,128)(2,1)}), bf16[16,32,512]{2,1,0:T(8,128)(2,1)S(1)}, u32[]{:S(2)}, u32[]{:S(2)}) async-start(bf16[16,32,512]{2,1,0:T(8,128)(2,1)} %bitcast.3), calls=%async_computation | async-start | bytes 1048576 | tf_op jit(solution)/shard_map/all_to_all | solution.py:42
  38.6 13.5 %copy-start.3 = (bf16[16,32,512]{2,1,0:T(8,128)(2,1)}, bf16[16,32,512]{2,1,0:T(8,128)(2,1)S(1)}, u32[]{:S(2)}) copy-start(bf16[16,32,512]{2,1,0:T(8,128)(2,1)S(1)} %all-to-all-done) | copy-start | bytes 1572868
  38.6 18.8 %all-to-all-start.2 = ((bf16[16,32,512]{2,1,0:T(8,128)(2,1)}), bf16[16,32,512]{2,1,0:T(8,128)(2,1)S(1)}, u32[]{:S(2)}, u32[]{:S(2)}) async-start(bf16[16,32,512]{2,1,0:T(8,128)(2,1)} %bitcast.13), calls=%async_computation.2 | async-start | bytes 1048576 | tf_op jit(solution)/shard_map/all_to_all | solution.py:43
  42.1 100.2 %reduce-scatter.7.cloned.1.call-start = ((), (), s32[]{:S(2)}) async-start(), calls=%async_computation.9 | async-start | bytes 2621440
  52.1 40.4 %copy-start.1 = (bf16[8,2,32,1024]{3,2,0,1:T(8,128)(2,1)}, bf16[8,2,32,1024]{3,2,0,1:T(8,128)(2,1)S(1)}, u32[]{:S(2)}) copy-start(bf16[8,2,32,1024]{3,2,0,1:T(8,128)(2,1)S(1)} %get-tuple-element.18) | copy-start | bytes 3145732
  57.4 28.3 %copy-start.5 = (bf16[16,32,512]{2,1,0:T(8,128)(2,1)}, bf16[16,32,512]{2,1,0:T(8,128)(2,1)S(1)}, u32[]{:S(2)}) copy-start(bf16[16,32,512]{2,1,0:T(8,128)(2,1)S(1)} %all-to-all-done.2) | copy-start | bytes 1572868
  85.7 3.3 %copy-start.4 = (bf16[16,32,512]{2,1,0:T(8,128)(2,1)S(1)}, bf16[16,32,512]{2,1,0:T(8,128)(2,1)}, u32[]{:S(2)}) copy-start(bf16[16,32,512]{2,1,0:T(8,128)(2,1)} %copy-done.3) | copy-start | bytes 1572868
  89.0 1.0 copy-start.2
  92.4 1.0 copy-start.6
  92.5 73.7 %reduce-scatter.5.cloned.1.call-start = ((), (), s32[]{:S(2)}) async-start(), calls=%async_computation.8 | async-start | bytes 2621440 | tf_op jit(solution)/shard_map/reduce_scatter | solution.py:96
  95.6 8.2 %copy-start = (bf16[512,2,1024]{2,0,1:T(8,128)(2,1)S(1)}, bf16[512,2,1024]{2,0,1:T(8,128)(2,1)}, u32[]{:S(2)}) copy-start(bf16[512,2,1024]{2,0,1:T(8,128)(2,1)} %all-gather.3.cloned.1.call-done) | copy-start | bytes 6291460
  99.2 20.0 %all-to-all-start.1 = ((bf16[16,32,512]{2,1,0:T(8,128)(2,1)}), bf16[16,32,512]{2,1,0:T(8,128)(2,1)S(1)}, u32[]{:S(2)}, u32[]{:S(2)}) async-start(bf16[16,32,512]{2,1,0:T(8,128)(2,1)} %bitcast.11), calls=%async_computation.1 | async-start | bytes 1048576 | tf_op jit(solution)/shard_map/all_to_all | solution.py:77
  119.2 18.8 %all-to-all-start.3 = ((bf16[16,32,512]{2,1,0:T(8,128)(2,1)}), bf16[16,32,512]{2,1,0:T(8,128)(2,1)S(1)}, u32[]{:S(2)}, u32[]{:S(2)}) async-start(bf16[16,32,512]{2,1,0:T(8,128)(2,1)} %bitcast.19), calls=%async_computation.3 | async-start | bytes 1048576 | tf_op jit(solution)/shard_map/all_to_all | solution.py:78
  138.0 3.6 %copy-start.9 = (bf16[128,512]{1,0:T(8,128)(2,1)S(1)}, bf16[128,512]{1,0:T(8,128)(2,1)}, u32[]{:S(2)}) copy-start(bf16[128,512]{1,0:T(8,128)(2,1)} %param.8) | copy-start | bytes 393220
Sparse Core Ops, SparseCore 0:
  10.4 38.0 all-gather.2
  50.3 35.2 all-gather.4
  92.6 35.1 reduce-scatter.6
  130.9 35.1 reduce-scatter.4
where the time goes:
time: 175 us
  waiting for transfers between devices  99.4 us (57%)
  local copies, waits for them, and re-layouts  24.8 us (14%)
  starting transfers between devices  18.3 us (10%)
  matrix products  14.5 us (8%)
  between operations  14 us (8%)
  other arithmetic  3.57 us (2%)
    all_gather x1, waiting for transfers between devices, on_device(): lax.all_gather(weight_out, 'fsdp', axis=0, tiled=True)  28.3 us
    reduce_scatter x1, waiting for transfers between devices, on_device(): lax.psum_scatter(jnp.einsum('sech,secd->hed', part, grad_rows, preferred_...  21.4 us
    all_to_all x1, waiting for transfers between devices, on_device(): lax.all_to_all(returned_send, 'expert', split_axis=0, concat_axis=0, tile...  13.8 us
    all_to_all x1, waiting for transfers between devices, on_device(): lax.all_to_all(values_send, 'expert', split_axis=0, concat_axis=0, tiled=...  12.5 us
    unnamed x32, local copies, waits for them, and re-layouts  12.3 us
    all_to_all x1, waiting for transfers between devices, on_device(): lax.all_to_all(send_knots, 'expert', split_axis=0, concat_axis=0, tiled=T...  11.8 us
    all_to_all x1, starting transfers between devices, on_device(): lax.all_to_all(send_knots, 'expert', split_axis=0, concat_axis=0, tiled=T...  6.33 us
    all_gather x1, waiting for transfers between devices, on_device(): lax.all_gather(weight_in, 'fsdp', axis=0, tiled=True)  6.31 us
  transfers between devices with their start and end apart: 8, of which 7 were waited for; matrix products, arithmetic and copies ran while one was open for 18% of the time, Pallas kernels for 0%

commit v1 on v0

v1 whole, which is shorter than its diff:
```python
import functools
import math

import jax
import jax.numpy as jnp
from jax import lax
from jax.experimental import pallas as pl
from jax.experimental.pallas import tpu as pltpu
from jax.sharding import PartitionSpec as P

MESH = pl.DeviceIdType.MESH
BF = jnp.bfloat16
F32 = jnp.float32


def dot(left, right, left_dim, right_dim):
    return lax.dot_general(
        left, right, (((left_dim,), (right_dim,)), ((), ())), preferred_element_type=F32
    )


def kernel(
    sizes,
    states, rates, ids, gates, cotangent, w_in, w_out,
    defect, grad_states, grad_in, grad_out,
    tok_send, tok_recv, ret_send, ret_recv,
    full_in, full_out, part_in, part_out,
    first_in, first_out, sum_in, sum_out, second_in, second_out,
    acc_v, acc_r, picks,
    tok_ss, tok_rs, ret_ss, ret_rs,
    w_ss, w_rs, one_ss, one_rs, two_ss, two_rs,
):
    groups, fsdp, nx, ny, local, cap = sizes
    rows, feature = states.shape
    hidden_all = w_in.shape[2]
    hrows = w_out.shape[1]
    slots = groups * local * cap
    lines = groups * cap
    g = lax.axis_index("expert")
    f = lax.axis_index("fsdp")
    y, x = f // nx, lax.rem(f, nx)

    shards = (w_in, w_out)
    fulls = (full_in, full_out)
    parts = (part_in, part_out)
    firsts = (first_in, first_out)
    sums = (sum_in, sum_out)
    seconds = (second_in, second_out)
    outs = (grad_in, grad_out)
    counts = ((nx, ny), (ny, nx))
    mine = ((x, y), (y, x))

    def place(arr, a, b):
        return b * nx + a if arr == 0 else a * nx + b

    def peer(arr, i, j):
        (n1, n2), (a, b) = counts[arr], mine[arr]
        return lax.rem(a + i, n1), lax.rem(b + j, n2)

    def push(src, dst, send, recv, device):
        return pltpu.make_async_remote_copy(
            src_ref=src, dst_ref=dst, send_sem=send, recv_sem=recv,
            device_id=device, device_id_type=MESH,
        )

    barrier = pltpu.get_barrier_semaphore()

    def greet(o, carry):
        pl.semaphore_signal(
            barrier, inc=1, device_id={"expert": lax.rem(g + o, groups)}, device_id_type=MESH
        )
        return carry

    lax.fori_loop(1, groups, greet, 0)
    for arr in range(2):
        for i in range(1, counts[arr][0]):
            a, b = peer(arr, i, 0)
            pl.semaphore_signal(
                barrier, inc=1, device_id={"fsdp": place(arr, a, b)}, device_id_type=MESH
            )
    pl.semaphore_wait(barrier, groups - 1 + nx - 1 + ny - 1)

    def shard_copy(arr, e, source, own, a, b, slot):
        src = shards[arr].at[e] if own else fulls[arr].at[e, source]
        return push(
            src, fulls[arr].at[e, source], w_ss.at[arr, e, slot], w_rs.at[arr, e, source],
            {"fsdp": place(arr, a, b)},
        )

    def own_copies(arr, e):
        n1, n2 = counts[arr]
        copies = []
        for i in range(1, n1):
            copies.append(shard_copy(arr, e, f, True, *peer(arr, i, 0), i - 1))
        for j in range(1, n2):
            copies.append(shard_copy(arr, e, f, True, *peer(arr, 0, j), n1 - 1 + j - 1))
        return copies

    def forward_copies(arr, e, i):
        n1, n2 = counts[arr]
        source = place(arr, *peer(arr, i, 0))
        return [
            shard_copy(arr, e, source, False, *peer(arr, 0, j), n1 - 1 + i * (n2 - 1) + j - 1)
            for j in range(1, n2)
        ]

    def send_own(e):
        one, two = own_copies(0, e), own_copies(1, e)
        for left, right in zip(one, two):
            left.start()
            right.start()

    def await_shard(arr, e, source):
        shard_copy(arr, e, source, False, *peer(arr, 0, 1), 0).wait_recv()

    def forward(e):
        for arr in range(2):
            for i in range(1, counts[arr][0]):
                await_shard(arr, e, place(arr, *peer(arr, i, 0)))
                for copy in forward_copies(arr, e, i):
                    copy.start()

    def await_rest(e):
        for arr in range(2):
            n1, n2 = counts[arr]
            for j in range(1, n2):
                for i in range(n1):
                    await_shard(arr, e, place(arr, *peer(arr, i, j)))

    send_own(0)

    experts_all = groups * local
    id_f = ids[...].astype(F32)
    expert_iota = lax.broadcasted_iota(jnp.int32, (rows, experts_all), 1).astype(F32)
    hit = [(id_f[:, k:k + 1] == expert_iota).astype(F32) for k in range(2)]
    below = (
        lax.broadcasted_iota(jnp.int32, (rows, rows), 0)
        > lax.broadcasted_iota(jnp.int32, (rows, rows), 1)
    ).astype(F32).astype(BF)
    before = dot(below, (hit[0] + hit[1]).astype(BF), 1, 0)
    slot_iota = lax.broadcasted_iota(jnp.int32, (rows, slots), 1).astype(F32)
    cot = cotangent[...].astype(F32)
    grads_slot = None
    for k in range(2):
        slot = jnp.sum(hit[k] * before, axis=1, keepdims=True)
        pick = (id_f[:, k:k + 1] * cap + slot == slot_iota).astype(F32).astype(BF)
        picks[k] = pick
        descent = (-gates[:, k:k + 1] * cot).astype(BF)
        term = dot(pick, descent, 0, 0)
        grads_slot = term if grads_slot is None else grads_slot + term
    knots_slot = dot(picks[0] + picks[1], states[...], 0, 0)
    shape = (groups, local, cap, feature)
    tok_send[:, :, 0] = knots_slot.astype(BF).reshape(shape)
    tok_send[:, :, 1] = grads_slot.astype(BF).reshape(shape)

    def tok_copy(o):
        other = lax.rem(g + o, groups)
        return push(
            tok_send.at[other], tok_recv.at[g], tok_ss.at[other], tok_rs.at[g], {"expert": other}
        )

    def tok_arrival(o):
        other = lax.rem(g + o, groups)
        return push(
            tok_send.at[other], tok_recv.at[other], tok_ss.at[other], tok_rs.at[other],
            {"expert": other},
        )

    def over_groups(act):
        def body(o, carry):
            act(o)
            return carry

        lax.fori_loop(1, groups, body, 0)

    over_groups(lambda o: tok_copy(o).start())
    tok_recv[g] = tok_send[g]
    for arr in range(2):
        for e in range(local):
            fulls[arr][e, f] = shards[arr][e]

    def ret_copy(e, o):
        other = lax.rem(g + o, groups)
        return push(
            ret_send.at[other, e], ret_recv.at[g, e], ret_ss.at[other, e], ret_rs.at[g, e],
            {"expert": other},
        )

    def ret_arrival(e, o):
        other = lax.rem(g + o, groups)
        return push(
            ret_send.at[other, e], ret_recv.at[other, e], ret_ss.at[other, e], ret_rs.at[other, e],
            {"expert": other},
        )

    width = max(256, hrows)
    per = width // hrows

    def compute(e):
        acc_v[...] = jnp.zeros_like(acc_v)
        acc_r[...] = jnp.zeros_like(acc_r)

        def chunk(c, carry):
            knots = tok_recv[:, e, 0].reshape(lines, feature)
            grads = tok_recv[:, e, 1].reshape(lines, feature)
            columns = pl.ds(pl.multiple_of(c * width, width), width)
            wi = full_in[e, :, :, columns].reshape(feature, width)
            wo = full_out[e, pl.ds(c * per, per)].reshape(width, feature)
            preact = dot(knots, wi, 1, 0)
            slope = dot(grads, wo, 1, 1)
            sigma = jax.nn.sigmoid(preact)
            hidden = (preact * sigma).astype(BF)
            inner = (slope * (sigma * (1.0 + preact * (1.0 - sigma)))).astype(BF)
            part_in[e, :, :, columns] = dot(knots, inner, 0, 0).astype(BF).reshape(
                fsdp, feature // fsdp, width
            )
            part_out[e, pl.ds(c * per, per)] = dot(hidden, grads, 0, 0).astype(BF).reshape(
                per, hrows, feature
            )
            acc_v[...] += dot(hidden, wo, 1, 0)
            acc_r[...] += dot(inner, wi, 1, 1)
            return carry

        lax.fori_loop(0, hidden_all // width, chunk, 0)
        back = (groups, cap, feature)
        ret_send[:, e, 0] = acc_v[...].astype(BF).reshape(back)
        ret_send[:, e, 1] = acc_r[...].astype(BF).reshape(back)

    def one_copy(arr, e, i, j):
        a, b = mine[arr]
        to, row = peer(arr, i, j)
        return push(
            parts[arr].at[e, place(arr, to, row)], firsts[arr].at[e, a, row],
            one_ss.at[arr, e, to, row], one_rs.at[arr, e, a, row],
            {"fsdp": place(arr, to, b)},
        )

    def one_arrival(arr, e, i, j):
        b = mine[arr][1]
        to, row = peer(arr, i, j)
        return push(
            parts[arr].at[e, place(arr, to, row)], firsts[arr].at[e, to, row],
            one_ss.at[arr, e, to, row], one_rs.at[arr, e, to, row],
            {"fsdp": place(arr, to, b)},
        )

    def two_copy(arr, e, j):
        a, b = mine[arr]
        row = peer(arr, 0, j)[1]
        return push(
            sums[arr].at[e, row], seconds[arr].at[e, b],
            two_ss.at[arr, e, row], two_rs.at[arr, e, b], {"fsdp": place(arr, a, row)},
        )

    def two_arrival(arr, e, j):
        a = mine[arr][0]
        row = peer(arr, 0, j)[1]
        return push(
            sums[arr].at[e, row], seconds[arr].at[e, row],
            two_ss.at[arr, e, row], two_rs.at[arr, e, row], {"fsdp": place(arr, a, row)},
        )

    def send_one(e):
        for j in list(range(1, max(nx, ny))) + [0]:
            for arr in range(2):
                n1, n2 = counts[arr]
                if j < n2:
                    for i in range(1, n1):
                        one_copy(arr, e, i, j).start()

    def summed(arr, e, j):
        a = mine[arr][0]
        row = peer(arr, 0, j)[1]
        total = parts[arr][e, place(arr, a, row)].astype(F32)
        for i in range(1, counts[arr][0]):
            one_arrival(arr, e, i, j).wait_recv()
            total = total + firsts[arr][e, peer(arr, i, 0)[0], row].astype(F32)
        return total

    def send_two(e):
        for arr in range(2):
            for j in range(1, counts[arr][1]):
                row = peer(arr, 0, j)[1]
                sums[arr][e, row] = summed(arr, e, j).astype(BF)
                two_copy(arr, e, j).start()

    def finish(e):
        for arr in range(2):
            total = summed(arr, e, 0)
            for j in range(1, counts[arr][1]):
                row = peer(arr, 0, j)[1]
                two_arrival(arr, e, j).wait_recv()
                total = total + seconds[arr][e, row].astype(F32)
            outs[arr][e] = total.astype(BF)

    forward(0)
    if local > 1:
        send_own(1)
    over_groups(lambda o: tok_arrival(o).wait_recv())
    for e in range(local):
        await_rest(e)
        compute(e)
        ret_recv[g, e] = ret_send[g, e]
        over_groups(lambda o: ret_copy(e, o).start())
        if e + 1 < local:
            forward(e + 1)
        send_one(e)
        if e + 2 < local:
            send_own(e + 2)
        if e >= 1:
            send_two(e - 1)
    send_two(local - 1)

    for e in range(local):
        over_groups(lambda o: ret_arrival(e, o).wait_recv())
    values = ret_recv[:, :, 0].reshape(slots, feature)
    combined = None
    for k in range(2):
        term = gates[:, k:k + 1] * dot(picks[k], values, 1, 0)
        combined = term if combined is None else combined + term
    defect[...] = (rates[...].astype(F32) - combined).astype(BF)
    returned = ret_recv[:, :, 1].reshape(slots, feature)
    grad_states[...] = dot(picks[0] + picks[1], returned, 1, 0).astype(BF)

    for e in range(local):
        finish(e)

    over_groups(lambda o: tok_copy(o).wait_send())
    for e in range(local):
        over_groups(lambda o: ret_copy(e, o).wait_send())
        for arr in range(2):
            n1, n2 = counts[arr]
            for copy in own_copies(arr, e):
                copy.wait_send()
            for i in range(1, n1):
                for copy in forward_copies(arr, e, i):
                    copy.wait_send()
                for j in range(n2):
                    one_copy(arr, e, i, j).wait_send()
            for j in range(1, n2):
                two_copy(arr, e, j).wait_send()


def on_device(states, rates, expert_ids, gate_weights, cotangent, weight_in, weight_out):
    groups, fsdp = lax.axis_size("expert"), lax.axis_size("fsdp")
    rows, feature = states.shape
    drows, local, hidden = weight_in.shape
    hrows = weight_out.shape[0]
    capacity = max(2, 4 * rows // (local * groups))
    cap = -(-capacity // 16) * 16
    nx = math.isqrt(fsdp)
    if nx * nx != fsdp:
        nx = fsdp
    ny = fsdp // nx
    slots = groups * local * cap
    w_in = jnp.transpose(weight_in, (1, 0, 2))
    w_out = jnp.transpose(weight_out, (1, 0, 2))
    shard_in, shard_out = (drows, hidden), (hrows, feature)
    exchange = (groups, local, 2, cap, feature)
    most = max(nx, ny)
    vmem = pl.BlockSpec(memory_space=pltpu.VMEM)
    dma = pltpu.SemaphoreType.DMA
    defect, grad_states, grad_in, grad_out = pl.pallas_call(
        functools.partial(kernel, (groups, fsdp, nx, ny, local, cap)),
        out_shape=(
            jax.ShapeDtypeStruct((rows, feature), BF),
            jax.ShapeDtypeStruct((rows, feature), BF),
            jax.ShapeDtypeStruct((local,) + shard_in, BF),
            jax.ShapeDtypeStruct((local,) + shard_out, BF),
        ),
        in_specs=[vmem] * 7,
        out_specs=(vmem,) * 4,
        scratch_shapes=[
            pltpu.VMEM(exchange, BF),
            pltpu.VMEM(exchange, BF),
            pltpu.VMEM(exchange, BF),
            pltpu.VMEM(exchange, BF),
            pltpu.VMEM((local, fsdp) + shard_in, BF),
            pltpu.VMEM((local, fsdp) + shard_out, BF),
            pltpu.VMEM((local, fsdp) + shard_in, BF),
            pltpu.VMEM((local, fsdp) + shard_out, BF),
            pltpu.VMEM((local, nx, ny) + shard_in, BF),
            pltpu.VMEM((local, ny, nx) + shard_out, BF),
            pltpu.VMEM((local, ny) + shard_in, BF),
            pltpu.VMEM((local, nx) + shard_out, BF),
            pltpu.VMEM((local, ny) + shard_in, BF),
            pltpu.VMEM((local, nx) + shard_out, BF),
            pltpu.VMEM((groups * cap, feature), F32),
            pltpu.VMEM((groups * cap, feature), F32),
            pltpu.VMEM((2, rows, slots), BF),
            dma((groups,)),
            dma((groups,)),
            dma((groups, local)),
            dma((groups, local)),
            dma((2, local, fsdp + most)),
            dma((2, local, fsdp)),
            dma((2, local, most, most)),
            dma((2, local, most, most)),
            dma((2, local, most)),
            dma((2, local, most)),
        ],
        compiler_params=pltpu.CompilerParams(
            collective_id=0, has_side_effects=True, vmem_limit_bytes=56 * 1024 * 1024
        ),
    )(states, rates, expert_ids, gate_weights, cotangent, w_in, w_out)
    return (
        defect,
        grad_states,
        jnp.transpose(grad_in, (1, 0, 2)),
        jnp.transpose(grad_out, (1, 0, 2)),
    )


def solution(mesh):
    placed = (
        P(("expert", "fsdp"), None),
        P(("expert", "fsdp"), None),
        P(("expert", "fsdp"), None),
        P(("expert", "fsdp"), None),
        P(("expert", "fsdp"), None),
        P("fsdp", "expert", None),
        P("fsdp", "expert", None),
    )
    return jax.shard_map(
        on_device,
        mesh=mesh,
        in_specs=placed,
        out_specs=(
            P(("expert", "fsdp"), None),
            P(("expert", "fsdp"), None),
            P("fsdp", "expert", None),
            P("fsdp", "expert", None),
        ),
        check_vma=False,
    )
```

time: 175 us -> 90.5 us (0.52)
  waiting for transfers between devices: 99.4 us -> 0 us
  Pallas kernels: 0 us -> 79.2 us
  starting transfers between devices: 18.3 us -> 0 us
  matrix products: 14.5 us -> 0 us
  local copies, waits for them, and re-layouts: 24.8 us -> 10.4 us
  between operations: 14 us -> 0.66 us
  other arithmetic: 3.57 us -> 0 us
    pallas_call x0 -> x1, Pallas kernels: none -> 79.2 us  [on_device(): pl.pallas_call(functools.partial(kernel, (groups, fsdp, nx, ny, local, ca...]
    all_to_all x4 -> x0, waiting for transfers between devices: 43.4 us -> none  [the longest x1 13.8 us: on_device(): lax.all_to_all(returned_send, 'expert', split_axis=0, concat_axis=0, tile...]
    all_gather x2 -> x0, waiting for transfers between devices: 34.6 us -> none  [the longest x1 28.3 us: on_device(): lax.all_gather(weight_out, 'fsdp', axis=0, tiled=True)]
    reduce_scatter x1 -> x0, waiting for transfers between devices: 21.4 us -> none  [on_device(): lax.psum_scatter(jnp.einsum('sech,secd->hed', part, grad_rows, preferred_...]
    all_to_all x4 -> x0, starting transfers between devices: 18.1 us -> none  [the longest x1 6.33 us: on_device(): lax.all_to_all(send_knots, 'expert', split_axis=0, concat_axis=0, tiled=T...]
    dot_general x6 -> x0, matrix products: 14.5 us -> none  [the longest x1 3.65 us: on_device(): jnp.einsum('secd,deh->sech', part, lax.all_gather(weight_in, 'fsdp', axis...]
    gather x4 -> x0, local copies, waits for them, and re-layouts: 7.57 us -> none  [the longest x1 2.64 us: on_device(): send_grads = padded_descent[source].reshape(send_shape)]
    reduce_sum x3 -> x0, other arithmetic: 2.11 us -> none  [the longest x1 1.33 us: on_device(): grad_states = jnp.sum(returned_knot, axis=1).astype(jnp.bfloat16)]
  transfers between devices with their start and end apart: 8 -> 0, of which waited for: 7 -> 0; matrix products, arithmetic and copies ran while one was open for 18% -> 0% of each run, Pallas kernels for 0% -> 0%
where the time goes in v1:
time: 90.5 us; the launch traced here: 90.2 us
  Pallas kernels  79.2 us (88%)
  local copies, waits for them, and re-layouts  10.4 us (11%)
    pallas_call x1, Pallas kernels, on_device(): pl.pallas_call(functools.partial(kernel, (groups, fsdp, nx, ny, local, ca...  79.2 us
    unnamed x18, local copies, waits for them, and re-layouts  10.4 us

profile of v1, /device:TPU:0, one launch (start us, length us, event | category | flops | bytes accessed | tf_op | source)
XLA Modules:
  0.0 90.2 jit_solution(15375714305801437676)
XLA Ops:
  0.6 0.0 copy-start.4
  0.6 1.4 %copy.13.ids = s32[128,2]{1,0:T(8,128)} copy(s32[128,2]{0,1:T(2,128)} %param.9) | data formatting | bytes 2048 | tf_op args[2]
  2.1 0.0 copy-done.4
  2.1 0.7 copy.14.gates
  2.8 0.0 copy-start
  2.8 2.0 %copy.20 = bf16[128,2,1024]{2,0,1:T(8,128)(2,1)} copy(bf16[128,2,1024]{2,1,0:T(2,128)(2,1)} %param.12) | data formatting | bytes 1048576 | tf_op args[5]
  4.8 0.0 copy-done
  4.8 0.8 copy.19
  5.7 79.2 %shard_map.102 = (bf16[128,512]{1,0:T(8,128)(2,1)}, bf16[128,512]{1,0:T(8,128)(2,1)}, bf16[2,128,1024]{2,1,0:T(8,128)(2,1)}, bf16[2,256,512]{2,1,0:T(8,128)(2,1)}) custom-call(bf16[128,512]{1,0:T(8,128)(2,1)} %states.1, bf16[128,512]{1,0:T(8,128)(2,1)} %rates.1, s32[128,2]{1,0:T(8,128)} %copy.13.ids, f32[128,2]{1,0:T(8,128)} %copy.14.gates, ...), custom_call_target="tpu_custom_call" | custom-call | tf_op jit(solution)/shard_map/pallas_call | solution.py:363
  84.8 0.0 copy-start.1
  84.8 2.4 %copy.15 = bf16[128,2,1024]{2,1,0:T(2,128)(2,1)} copy(bf16[128,2,1024]{2,0,1:T(8,128)(2,1)} %bitcast.11) | data formatting | bytes 1048576
  87.3 0.0 copy-done.1
  87.3 0.0 copy-start.3
  87.3 1.3 %copy.16 = bf16[256,2,512]{2,1,0:T(2,128)(2,1)} copy(bf16[256,2,512]{2,0,1:T(8,128)(2,1)S(1)} %bitcast.10) | data formatting | bytes 1048576
  88.6 0.0 copy-done.3
  88.6 0.0 copy-start.2
  88.6 0.7 copy.23
  89.3 0.3 copy-done.2
  89.6 0.7 copy.24
Async XLA Ops:
  0.6 1.4 %copy-start.4 = (f32[128,2]{0,1:T(2,128)S(1)}, f32[128,2]{0,1:T(2,128)}, u32[]{:S(2)}) copy-start(f32[128,2]{0,1:T(2,128)} %param.10) | copy-start | bytes 3076
  2.8 2.0 %copy-start = (bf16[256,2,512]{2,1,0:T(2,128)(2,1)S(1)}, bf16[256,2,512]{2,1,0:T(2,128)(2,1)}, u32[]{:S(2)}) copy-start(bf16[256,2,512]{2,1,0:T(2,128)(2,1)} %param.13) | copy-start | bytes 1572868
  84.8 2.4 %copy-start.1 = (bf16[2,256,512]{2,1,0:T(8,128)(2,1)S(1)}, bf16[2,256,512]{2,1,0:T(8,128)(2,1)}, u32[]{:S(2)}) copy-start(bf16[2,256,512]{2,1,0:T(8,128)(2,1)} %get-tuple-element.11) | copy-start | bytes 1572868
  87.3 1.3 %copy-start.3 = (bf16[128,512]{1,0:T(8,128)(2,1)S(1)}, bf16[128,512]{1,0:T(8,128)(2,1)}, u32[]{:S(2)}) copy-start(bf16[128,512]{1,0:T(8,128)(2,1)} %get-tuple-element.20) | copy-start | bytes 393220
  88.6 1.0 %copy-start.2 = (bf16[128,512]{1,0:T(8,128)(2,1)S(1)}, bf16[128,512]{1,0:T(8,128)(2,1)}, u32[]{:S(2)}) copy-start(bf16[128,512]{1,0:T(8,128)(2,1)} %get-tuple-element.21) | copy-start | bytes 393220

commit v2 on v0

v2 whole, which is shorter than its diff:
```python
import functools
import math

import jax
import jax.numpy as jnp
from jax import lax
from jax.experimental import pallas as pl
from jax.experimental.pallas import tpu as pltpu
from jax.sharding import PartitionSpec as P

MESH = pl.DeviceIdType.MESH
BF = jnp.bfloat16
F32 = jnp.float32


def dot(left, right, left_dim, right_dim):
    return lax.dot_general(
        left, right, (((left_dim,), (right_dim,)), ((), ())), preferred_element_type=F32
    )


def kernel(
    sizes,
    states, rates, ids, gates, cotangent, w_in, w_out,
    defect, grad_states, grad_in, grad_out,
    tok_send, tok_recv, ret_send, ret_recv,
    full_in, full_out, part_in, part_out,
    first_in, first_out, sum_in, sum_out, second_in, second_out,
    acc_v, acc_r, picks,
    tok_ss, tok_rs, ret_ss, ret_rs,
    w_ss, w_rs, one_ss, one_rs, two_ss, two_rs,
):
    groups, fsdp, nx, ny, local, cap = sizes
    rows, feature = states.shape
    hidden_all = w_in.shape[2]
    hrows = w_out.shape[1]
    slots = groups * local * cap
    lines = local * groups * cap
    sets = nx // local
    g = lax.axis_index("expert")
    f = lax.axis_index("fsdp")
    y, x = f // nx, lax.rem(f, nx)
    q, mine = x // local, lax.rem(x, local)
    span = hidden_all // ny

    shards = (w_in, w_out)
    fulls = (full_in, full_out)
    parts = (part_in, part_out)
    firsts = (first_in, first_out)
    sums = (sum_in, sum_out)
    seconds = (second_in, second_out)
    outs = (grad_in, grad_out)

    def turn(own, step, size):
        return lax.rem(own + step, size)

    def push(src, dst, send, recv, **device):
        return pltpu.make_async_remote_copy(
            src_ref=src, dst_ref=dst, send_sem=send, recv_sem=recv,
            device_id=device, device_id_type=MESH,
        )

    def greet(**device):
        pl.semaphore_signal(barrier, inc=1, device_id=device, device_id_type=MESH)

    def over_groups(start, act):
        def body(o, carry):
            act(o)
            return carry

        lax.fori_loop(start, groups, body, 0)

    def over_peers(act):
        for d in range(local):
            over_groups(1 if d == 0 else 0, functools.partial(act, d))

    barrier = pltpu.get_barrier_semaphore()
    over_peers(
        lambda d, o: greet(
            expert=turn(g, o, groups), fsdp=y * nx + q * local + turn(mine, d, local)
        )
    )
    for k in range(1, sets):
        for d in range(local):
            greet(fsdp=y * nx + turn(q, k, sets) * local + d)
    for j in range(1, ny):
        greet(fsdp=turn(y, j, ny) * nx + x)
    pl.semaphore_wait(barrier, groups * local - 1 + nx - local + ny - 1)

    def along_x(arr, i):
        to = turn(x, i, nx)
        return push(
            shards[arr].at[lax.rem(to, local)], fulls[arr].at[f],
            w_ss.at[arr, i - 1], w_rs.at[arr, f], fsdp=y * nx + to,
        )

    def along_y(arr, i, j):
        source = y * nx + turn(x, i, nx)
        src = shards[arr].at[mine] if i == 0 else fulls[arr].at[source]
        return push(
            src, fulls[arr].at[source], w_ss.at[arr, nx - 1 + i * (ny - 1) + j - 1],
            w_rs.at[arr, source], fsdp=turn(y, j, ny) * nx + x,
        )

    def shard_arrival(arr, i, j):
        source = turn(y, j, ny) * nx + turn(x, i, nx)
        return push(
            fulls[arr].at[source], fulls[arr].at[source], w_ss.at[arr, 0], w_rs.at[arr, source],
            fsdp=turn(y, j, ny) * nx + (x if j else turn(x, i, nx)),
        )

    for arr in range(2):
        for i in range(1, nx):
            along_x(arr, i).start()
        for j in range(1, ny):
            along_y(arr, 0, j).start()

    experts_all = groups * local
    id_f = ids[...].astype(F32)
    gate = gates[...].T
    expert_iota = lax.broadcasted_iota(jnp.int32, (experts_all, rows), 0).astype(F32)
    hit = [(id_f[k:k + 1] == expert_iota).astype(F32) for k in range(2)]
    above = (
        lax.broadcasted_iota(jnp.int32, (rows, rows), 0)
        < lax.broadcasted_iota(jnp.int32, (rows, rows), 1)
    ).astype(F32).astype(BF)
    before = dot((hit[0] + hit[1]).astype(BF), above, 1, 0)
    slot_iota = lax.broadcasted_iota(jnp.int32, (slots, rows), 0).astype(F32)
    cot = cotangent[...].astype(F32)
    grads_slot = None
    for k in range(2):
        slot = jnp.sum(hit[k] * before, axis=0, keepdims=True)
        pick = (id_f[k:k + 1] * cap + slot == slot_iota).astype(F32).astype(BF)
        picks[k] = pick
        descent = (-gate[:, k:k + 1] * cot).astype(BF)
        term = dot(pick, descent, 1, 0)
        grads_slot = term if grads_slot is None else grads_slot + term
    shape = (groups, local, cap, feature)
    tok_send[:, :, 1] = grads_slot.astype(BF).reshape(shape)
    knots_slot = dot(picks[0] + picks[1], states[...], 1, 0)
    tok_send[:, :, 0] = knots_slot.astype(BF).reshape(shape)

    def tok_copy(d, o):
        other, e = turn(g, o, groups), turn(mine, d, local)
        return push(
            tok_send.at[other, e], tok_recv.at[mine, g], tok_ss.at[other, e], tok_rs.at[mine, g],
            expert=other, fsdp=y * nx + q * local + e,
        )

    def tok_arrival(d, o):
        other, e = turn(g, o, groups), turn(mine, d, local)
        return push(
            tok_send.at[other, e], tok_recv.at[e, other], tok_ss.at[other, e], tok_rs.at[e, other],
            expert=other, fsdp=y * nx + q * local + e,
        )

    over_peers(lambda d, o: tok_copy(d, o).start())
    tok_recv[mine, g] = tok_send[g, mine]
    for arr in range(2):
        fulls[arr][f] = shards[arr][mine]

    for arr in range(2):
        for i in range(1, nx):
            shard_arrival(arr, i, 0).wait_recv()
            for j in range(1, ny):
                along_y(arr, i, j).start()
    over_peers(lambda d, o: tok_arrival(d, o).wait_recv())
    for arr in range(2):
        for j in range(1, ny):
            for i in range(nx):
                shard_arrival(arr, i, j).wait_recv()

    width = max(256, hrows)
    per = width // hrows
    steps = span // width

    def one_copy(arr, j, i, row):
        there, column = turn(y, j, ny), turn(x, i, nx)
        shard = there * nx + column
        if arr == 1:
            return push(
                part_out.at[shard], first_out.at[y, column],
                one_ss.at[1, there, column, 0], one_rs.at[1, y, column, 0],
                fsdp=there * nx + x,
            )
        place = pl.ds(pl.multiple_of(row * span, span), span)
        return push(
            part_in.at[shard, :, place], first_in.at[y, column, :, place],
            one_ss.at[0, there, column, row], one_rs.at[0, y, column, row],
            fsdp=there * nx + x,
        )

    def one_arrival(arr, j, i, row):
        there, column = turn(y, j, ny), turn(x, i, nx)
        shard = there * nx + column
        if arr == 1:
            return push(
                part_out.at[shard], first_out.at[there, column],
                one_ss.at[1, there, column, 0], one_rs.at[1, there, column, 0],
                fsdp=there * nx + x,
            )
        place = pl.ds(pl.multiple_of(row * span, span), span)
        return push(
            part_in.at[shard, :, place], first_in.at[there, column, :, place],
            one_ss.at[0, there, column, row], one_rs.at[0, there, column, row],
            fsdp=there * nx + x,
        )

    acc_v[...] = jnp.zeros_like(acc_v)
    acc_r[...] = jnp.zeros_like(acc_r)
    for stage in range(1, ny + 1):
        row = turn(y, stage, ny)

        def chunk(c, carry):
            knots = tok_recv[:, :, 0].reshape(lines, feature)
            grads = tok_recv[:, :, 1].reshape(lines, feature)
            at = row * steps + c
            columns = pl.ds(pl.multiple_of(at * width, width), width)
            wi = full_in[:, :, columns].reshape(feature, width)
            wo = full_out[pl.ds(at * per, per)].reshape(width, feature)
            preact = dot(knots, wi, 1, 0)
            slope = dot(grads, wo, 1, 1)
            sigma = jax.nn.sigmoid(preact)
            hidden = (preact * sigma).astype(BF)
            inner = (slope * (sigma * (1.0 + preact * (1.0 - sigma)))).astype(BF)
            part_in[:, :, columns] = dot(knots, inner, 0, 0).astype(BF).reshape(
                fsdp, feature // fsdp, width
            )
            part_out[pl.ds(at * per, per)] = dot(hidden, grads, 0, 0).astype(BF).reshape(
                per, hrows, feature
            )
            acc_v[...] += dot(hidden, wo, 1, 0)
            acc_r[...] += dot(inner, wi, 1, 1)
            return carry

        lax.fori_loop(0, steps, chunk, 0)
        for i in list(range(1, nx)) + [0]:
            if stage < ny:
                one_copy(1, stage, i, 0).start()
            for j in range(1, ny):
                one_copy(0, j, i, row).start()

    back = (local, groups, cap, feature)
    ret_send[:, :, 0] = acc_v[...].astype(BF).reshape(back)
    ret_send[:, :, 1] = acc_r[...].astype(BF).reshape(back)

    def ret_copy(d, o):
        other, c = turn(g, o, groups), turn(mine, d, local)
        return push(
            ret_send.at[c, other], ret_recv.at[g, mine], ret_ss.at[c, other], ret_rs.at[g, mine],
            expert=other, fsdp=y * nx + q * local + c,
        )

    def ret_arrival(d, o):
        other, c = turn(g, o, groups), turn(mine, d, local)
        return push(
            ret_send.at[c, other], ret_recv.at[other, c], ret_ss.at[c, other], ret_rs.at[other, c],
            expert=other, fsdp=y * nx + q * local + c,
        )

    over_peers(lambda d, o: ret_copy(d, o).start())
    ret_recv[g, mine] = ret_send[mine, g]

    def two_copy(arr, i):
        to = turn(x, i, nx)
        return push(
            sums[arr].at[to], seconds[arr].at[x], two_ss.at[arr, to], two_rs.at[arr, x],
            fsdp=y * nx + to,
        )

    def two_arrival(arr, source):
        return push(
            sums[arr].at[source], seconds[arr].at[source], two_ss.at[arr, source],
            two_rs.at[arr, source], fsdp=y * nx + source,
        )

    def summed(arr, i):
        column = turn(x, i, nx)
        total = parts[arr][y * nx + column].astype(F32)
        for j in range(1, ny):
            for row in range(ny if arr == 0 else 1):
                one_arrival(arr, j, i, row).wait_recv()
            total = total + firsts[arr][turn(y, j, ny), column].astype(F32)
        return total

    for i in range(1, nx):
        for arr in (1, 0):
            sums[arr][turn(x, i, nx)] = summed(arr, i).astype(BF)
            two_copy(arr, i).start()
    own = [summed(arr, 0) for arr in range(2)]
    for arr in range(2):
        total = own[arr]
        for k in range(1, sets):
            source = turn(q, k, sets) * local + mine
            two_arrival(arr, source).wait_recv()
            total = total + seconds[arr][source].astype(F32)
        outs[arr][mine] = total.astype(BF)

    over_peers(lambda d, o: ret_arrival(d, o).wait_recv())
    values = ret_recv[:, :, 0].reshape(slots, feature)
    combined = None
    for k in range(2):
        term = gate[:, k:k + 1] * dot(picks[k], values, 0, 0)
        combined = term if combined is None else combined + term
    defect[...] = (rates[...].astype(F32) - combined).astype(BF)
    returned = ret_recv[:, :, 1].reshape(slots, feature)
    grad_states[...] = dot(picks[0] + picks[1], returned, 0, 0).astype(BF)

    for d in range(1, local):
        e = turn(mine, d, local)
        for arr in (1, 0):
            total = None
            for k in range(sets):
                source = turn(q, k, sets) * local + e
                two_arrival(arr, source).wait_recv()
                term = seconds[arr][source].astype(F32)
                total = term if total is None else total + term
            outs[arr][e] = total.astype(BF)

    over_peers(lambda d, o: tok_copy(d, o).wait_send())
    over_peers(lambda d, o: ret_copy(d, o).wait_send())
    for arr in range(2):
        for i in range(1, nx):
            along_x(arr, i).wait_send()
            two_copy(arr, i).wait_send()
        for j in range(1, ny):
            for i in range(nx):
                along_y(arr, i, j).wait_send()
                for row in range(ny if arr == 0 else 1):
                    one_copy(arr, j, i, row).wait_send()


def on_device(states, rates, expert_ids, gate_weights, cotangent, weight_in, weight_out):
    groups, fsdp = lax.axis_size("expert"), lax.axis_size("fsdp")
    rows, feature = states.shape
    drows, local, hidden = weight_in.shape
    hrows = weight_out.shape[0]
    capacity = max(2, 4 * rows // (local * groups))
    cap = -(-capacity // 16) * 16
    nx = math.isqrt(fsdp)
    ny = fsdp // nx
    slots = groups * local * cap
    w_in = jnp.transpose(weight_in, (1, 0, 2))
    w_out = jnp.transpose(weight_out, (1, 0, 2))
    shard_in, shard_out = (drows, hidden), (hrows, feature)
    exchange = (groups, local, 2, cap, feature)
    swapped = (local, groups, 2, cap, feature)
    vmem = pl.BlockSpec(memory_space=pltpu.VMEM)
    dma = pltpu.SemaphoreType.DMA
    defect, grad_states, grad_in, grad_out = pl.pallas_call(
        functools.partial(kernel, (groups, fsdp, nx, ny, local, cap)),
        out_shape=(
            jax.ShapeDtypeStruct((rows, feature), BF),
            jax.ShapeDtypeStruct((rows, feature), BF),
            jax.ShapeDtypeStruct((local,) + shard_in, BF),
            jax.ShapeDtypeStruct((local,) + shard_out, BF),
        ),
        in_specs=[vmem] * 7,
        out_specs=(vmem,) * 4,
        scratch_shapes=[
            pltpu.VMEM(exchange, BF),
            pltpu.VMEM(swapped, BF),
            pltpu.VMEM(swapped, BF),
            pltpu.VMEM(exchange, BF),
            pltpu.VMEM((fsdp,) + shard_in, BF),
            pltpu.VMEM((fsdp,) + shard_out, BF),
            pltpu.VMEM((fsdp,) + shard_in, BF),
            pltpu.VMEM((fsdp,) + shard_out, BF),
            pltpu.VMEM((ny, nx) + shard_in, BF),
            pltpu.VMEM((ny, nx) + shard_out, BF),
            pltpu.VMEM((nx,) + shard_in, BF),
            pltpu.VMEM((nx,) + shard_out, BF),
            pltpu.VMEM((nx,) + shard_in, BF),
            pltpu.VMEM((nx,) + shard_out, BF),
            pltpu.VMEM((local * groups * cap, feature), F32),
            pltpu.VMEM((local * groups * cap, feature), F32),
            pltpu.VMEM((2, slots, rows), BF),
            dma((groups, local)),
            dma((local, groups)),
            dma((local, groups)),
            dma((groups, local)),
            dma((2, fsdp + nx)),
            dma((2, fsdp)),
            dma((2, ny, nx, ny)),
            dma((2, ny, nx, ny)),
            dma((2, nx)),
            dma((2, nx)),
        ],
        compiler_params=pltpu.CompilerParams(
            collective_id=0, has_side_effects=True, vmem_limit_bytes=56 * 1024 * 1024
        ),
    )(states, rates, expert_ids.T, gate_weights.T, cotangent, w_in, w_out)
    return (
        defect,
        grad_states,
        jnp.transpose(grad_in, (1, 0, 2)),
        jnp.transpose(grad_out, (1, 0, 2)),
    )


def solution(mesh):
    placed = (
        P(("expert", "fsdp"), None),
        P(("expert", "fsdp"), None),
        P(("expert", "fsdp"), None),
        P(("expert", "fsdp"), None),
        P(("expert", "fsdp"), None),
        P("fsdp", "expert", None),
        P("fsdp", "expert", None),
    )
    return jax.shard_map(
        on_device,
        mesh=mesh,
        in_specs=placed,
        out_specs=(
            P(("expert", "fsdp"), None),
            P(("expert", "fsdp"), None),
            P("fsdp", "expert", None),
            P("fsdp", "expert", None),
        ),
        check_vma=False,
    )
```

time: 175 us -> 75.6 us (0.43)
  waiting for transfers between devices: 99.4 us -> 0 us
  Pallas kernels: 0 us -> 66.5 us
  starting transfers between devices: 18.3 us -> 0 us
  local copies, waits for them, and re-layouts: 24.8 us -> 8.24 us
  matrix products: 14.5 us -> 0 us
  between operations: 14 us -> 0.66 us
  other arithmetic: 3.57 us -> 0 us
    pallas_call x0 -> x1, Pallas kernels: none -> 66.5 us  [on_device(): pl.pallas_call(functools.partial(kernel, (groups, fsdp, nx, ny, local, ca...]
    all_to_all x4 -> x0, waiting for transfers between devices: 43.4 us -> none  [the longest x1 13.8 us: on_device(): lax.all_to_all(returned_send, 'expert', split_axis=0, concat_axis=0, tile...]
    all_gather x2 -> x0, waiting for transfers between devices: 34.6 us -> none  [the longest x1 28.3 us: on_device(): lax.all_gather(weight_out, 'fsdp', axis=0, tiled=True)]
    reduce_scatter x1 -> x0, waiting for transfers between devices: 21.4 us -> none  [on_device(): lax.psum_scatter(jnp.einsum('sech,secd->hed', part, grad_rows, preferred_...]
    all_to_all x4 -> x0, starting transfers between devices: 18.1 us -> none  [the longest x1 6.33 us: on_device(): lax.all_to_all(send_knots, 'expert', split_axis=0, concat_axis=0, tiled=T...]
    dot_general x6 -> x0, matrix products: 14.5 us -> none  [the longest x1 3.65 us: on_device(): jnp.einsum('secd,deh->sech', part, lax.all_gather(weight_in, 'fsdp', axis...]
    gather x4 -> x0, local copies, waits for them, and re-layouts: 7.57 us -> none  [the longest x1 2.64 us: on_device(): send_grads = padded_descent[source].reshape(send_shape)]
    unnamed x32 -> x14, local copies, waits for them, and re-layouts: 12.3 us -> 8.24 us
  transfers between devices with their start and end apart: 8 -> 0, of which waited for: 7 -> 0; matrix products, arithmetic and copies ran while one was open for 18% -> 0% of each run, Pallas kernels for 0% -> 0%
where the time goes in v2:
time: 75.6 us; the launch traced here: 75.4 us
  Pallas kernels  66.5 us (88%)
  local copies, waits for them, and re-layouts  8.24 us (11%)
    pallas_call x1, Pallas kernels, on_device(): pl.pallas_call(functools.partial(kernel, (groups, fsdp, nx, ny, local, ca...  66.5 us
    unnamed x14, local copies, waits for them, and re-layouts  8.24 us

profile of v2, /device:TPU:0, one launch (start us, length us, event | category | flops | bytes accessed | tf_op | source)
XLA Modules:
  0.0 75.4 jit_solution(6667890350482608830)
XLA Ops:
  0.6 0.0 copy-start
  0.6 2.0 %copy.18 = bf16[128,2,1024]{2,0,1:T(8,128)(2,1)} copy(bf16[128,2,1024]{2,1,0:T(2,128)(2,1)} %param.12) | data formatting | bytes 1048576 | tf_op args[5]
  2.7 0.0 copy-done
  2.7 0.8 %copy.17 = bf16[256,2,512]{2,0,1:T(8,128)(2,1)} copy(bf16[256,2,512]{2,1,0:T(2,128)(2,1)S(1)} %copy-done) | data formatting | bytes 1048576 | tf_op args[6]
  3.5 66.5 %shard_map.102 = (bf16[128,512]{1,0:T(8,128)(2,1)}, bf16[128,512]{1,0:T(8,128)(2,1)}, bf16[2,128,1024]{2,1,0:T(8,128)(2,1)}, bf16[2,256,512]{2,1,0:T(8,128)(2,1)}) custom-call(bf16[128,512]{1,0:T(8,128)(2,1)} %states.1, bf16[128,512]{1,0:T(8,128)(2,1)} %rates.1, s32[2,128]{1,0:T(2,128)} %bitcast.14, f32[2,128]{1,0:T(2,128)} %bitcast.15, ...), custom_call_target="tpu_custom_call" | custom-call | tf_op jit(solution)/shard_map/pallas_call | solution.py:350
  70.1 0.0 copy-start.1
  70.1 2.4 %copy.13 = bf16[128,2,1024]{2,1,0:T(2,128)(2,1)} copy(bf16[128,2,1024]{2,0,1:T(8,128)(2,1)} %bitcast.13) | data formatting | bytes 1048576
  72.5 0.0 copy-done.1
  72.5 0.0 copy-start.3
  72.5 1.3 %copy.14 = bf16[256,2,512]{2,1,0:T(2,128)(2,1)} copy(bf16[256,2,512]{2,0,1:T(8,128)(2,1)S(1)} %bitcast.12) | data formatting | bytes 1048576
  73.8 0.0 copy-done.3
  73.8 0.0 copy-start.2
  73.8 0.7 copy.21
  74.5 0.3 copy-done.2
  74.8 0.7 copy.22
Async XLA Ops:
  0.6 2.0 %copy-start = (bf16[256,2,512]{2,1,0:T(2,128)(2,1)S(1)}, bf16[256,2,512]{2,1,0:T(2,128)(2,1)}, u32[]{:S(2)}) copy-start(bf16[256,2,512]{2,1,0:T(2,128)(2,1)} %param.13) | copy-start | bytes 1572868
  70.1 2.4 %copy-start.1 = (bf16[2,256,512]{2,1,0:T(8,128)(2,1)S(1)}, bf16[2,256,512]{2,1,0:T(8,128)(2,1)}, u32[]{:S(2)}) copy-start(bf16[2,256,512]{2,1,0:T(8,128)(2,1)} %get-tuple-element.11) | copy-start | bytes 1572868
  72.5 1.3 %copy-start.3 = (bf16[128,512]{1,0:T(8,128)(2,1)S(1)}, bf16[128,512]{1,0:T(8,128)(2,1)}, u32[]{:S(2)}) copy-start(bf16[128,512]{1,0:T(8,128)(2,1)} %get-tuple-element.20) | copy-start | bytes 393220
  73.8 1.0 %copy-start.2 = (bf16[128,512]{1,0:T(8,128)(2,1)S(1)}, bf16[128,512]{1,0:T(8,128)(2,1)}, u32[]{:S(2)}) copy-start(bf16[128,512]{1,0:T(8,128)(2,1)} %get-tuple-element.21) | copy-start | bytes 393220

commit v3 on v2

--- a/solution.py
+++ b/solution.py
@@ -26,7 +26,7 @@
     tok_send, tok_recv, ret_send, ret_recv,
     full_in, full_out, part_in, part_out,
     first_in, first_out, sum_in, sum_out, second_in, second_out,
-    acc_v, acc_r, picks,
+    acc_v, acc_r, picks, knots_t,
     tok_ss, tok_rs, ret_ss, ret_rs,
     w_ss, w_rs, one_ss, one_rs, two_ss, two_rs,
 ):
@@ -70,8 +70,8 @@
 
         lax.fori_loop(start, groups, body, 0)
 
-    def over_peers(act):
-        for d in range(local):
+    def over_peers(act, order=1):
+        for d in range(local)[::order]:
             over_groups(1 if d == 0 else 0, functools.partial(act, d))
 
     barrier = pltpu.get_barrier_semaphore()
@@ -85,8 +85,6 @@
             greet(fsdp=y * nx + turn(q, k, sets) * local + d)
     for j in range(1, ny):
         greet(fsdp=turn(y, j, ny) * nx + x)
-    pl.semaphore_wait(barrier, groups * local - 1 + nx - local + ny - 1)
-
     def along_x(arr, i):
         to = turn(x, i, nx)
         return push(
@@ -108,12 +106,6 @@
             fulls[arr].at[source], fulls[arr].at[source], w_ss.at[arr, 0], w_rs.at[arr, source],
             fsdp=turn(y, j, ny) * nx + (x if j else turn(x, i, nx)),
         )
-
-    for arr in range(2):
-        for i in range(1, nx):
-            along_x(arr, i).start()
-        for j in range(1, ny):
-            along_y(arr, 0, j).start()
 
     experts_all = groups * local
     id_f = ids[...].astype(F32)
@@ -154,6 +146,13 @@
             expert=other, fsdp=y * nx + q * local + e,
         )
 
+    pl.semaphore_wait(barrier, groups * local - 1 + nx - local + ny - 1)
+
+    for arr in range(2):
+        for i in range(1, nx):
+            along_x(arr, i).start()
+        for j in range(1, ny):
+            along_y(arr, 0, j).start()
     over_peers(lambda d, o: tok_copy(d, o).start())
     tok_recv[mine, g] = tok_send[g, mine]
     for arr in range(2):
@@ -206,6 +205,7 @@
             fsdp=there * nx + x,
         )
 
+    knots_t[...] = tok_recv[:, :, 0].reshape(lines, feature).T
     acc_v[...] = jnp.zeros_like(acc_v)
     acc_r[...] = jnp.zeros_like(acc_r)
     for stage in range(1, ny + 1):
@@ -223,7 +223,7 @@
             sigma = jax.nn.sigmoid(preact)
             hidden = (preact * sigma).astype(BF)
             inner = (slope * (sigma * (1.0 + preact * (1.0 - sigma)))).astype(BF)
-            part_in[:, :, columns] = dot(knots, inner, 0, 0).astype(BF).reshape(
+            part_in[:, :, columns] = dot(knots_t[...], inner, 1, 0).astype(BF).reshape(
                 fsdp, feature // fsdp, width
             )
             part_out[pl.ds(at * per, per)] = dot(hidden, grads, 0, 0).astype(BF).reshape(
@@ -234,12 +234,18 @@
             return carry
 
         lax.fori_loop(0, steps, chunk, 0)
-        for i in list(range(1, nx)) + [0]:
+        for i in range(1, nx):
             if stage < ny:
                 one_copy(1, stage, i, 0).start()
             for j in range(1, ny):
                 one_copy(0, j, i, row).start()
 
+    for stage in range(1, ny + 1):
+        for j in range(1, ny):
+            one_copy(0, j, 0, turn(y, stage, ny)).start()
+    for j in range(1, ny):
+        one_copy(1, j, 0, 0).start()
+
     back = (local, groups, cap, feature)
     ret_send[:, :, 0] = acc_v[...].astype(BF).reshape(back)
     ret_send[:, :, 1] = acc_r[...].astype(BF).reshape(back)
@@ -258,7 +264,7 @@
             expert=other, fsdp=y * nx + q * local + c,
         )
 
-    over_peers(lambda d, o: ret_copy(d, o).start())
+    over_peers(lambda d, o: ret_copy(d, o).start(), -1)
     ret_recv[g, mine] = ret_send[mine, g]
 
     def two_copy(arr, i):
@@ -375,6 +381,7 @@
             pltpu.VMEM((local * groups * cap, feature), F32),
             pltpu.VMEM((local * groups * cap, feature), F32),
             pltpu.VMEM((2, slots, rows), BF),
+            pltpu.VMEM((feature, local * groups * cap), BF),
             dma((groups, local)),
             dma((local, groups)),
             dma((local, groups)),
@@ -387,7 +394,7 @@
             dma((2, nx)),
         ],
         compiler_params=pltpu.CompilerParams(
-            collective_id=0, has_side_effects=True, vmem_limit_bytes=56 * 1024 * 1024
+            collective_id=0, has_side_effects=True, vmem_limit_bytes=36 * 1024 * 1024
         ),
     )(states, rates, expert_ids.T, gate_weights.T, cotangent, w_in, w_out)
     return (

time: 75.6 us -> 68.2 us (0.902)
  Pallas kernels: 66.5 us -> 61.1 us
  local copies, waits for them, and re-layouts: 8.24 us -> 6.18 us
    pallas_call x1, Pallas kernels: 66.5 us -> 61.1 us  [on_device(): pl.pallas_call(functools.partial(kernel, (groups, fsdp, nx, ny, local, ca...]
    unnamed x14 -> x18, local copies, waits for them, and re-layouts: 8.24 us -> 6.18 us
where the time goes in v3:
time: 68.2 us; the launch traced here: 68 us
  Pallas kernels  61.1 us (90%)
  local copies, waits for them, and re-layouts  6.18 us (9%)
  between operations  0.71 us (1%)
    pallas_call x1, Pallas kernels, on_device(): pl.pallas_call(functools.partial(kernel, (groups, fsdp, nx, ny, local, ca...  61.1 us
    unnamed x18, local copies, waits for them, and re-layouts  6.18 us

profile of v3, /device:TPU:0, one launch (start us, length us, event | category | flops | bytes accessed | tf_op | source)
XLA Modules:
  0.0 68.0 jit_solution(3155995472307934098)
XLA Ops:
  0.6 0.0 copy-start.5
  0.6 1.2 %copy.18 = bf16[128,2,1024]{2,0,1:T(8,128)(2,1)S(1)} copy(bf16[128,2,1024]{2,1,0:T(2,128)(2,1)} %param.12) | data formatting | bytes 1048576 | tf_op args[5]
  1.9 0.0 copy-done.5
  1.9 0.0 copy-start
  1.9 0.0 copy-start.1
  1.9 0.0 copy-start.2
  1.9 0.0 copy-start.4
  1.9 0.1 copy.17
  2.0 0.0 copy-start.3
  2.0 0.8 %copy-done = bf16[128,512]{1,0:T(8,128)(2,1)S(1)} copy-done((bf16[128,512]{1,0:T(8,128)(2,1)S(1)}, bf16[128,512]{1,0:T(8,128)(2,1)}, u32[]{:S(2)}) %copy-start) | copy-done | bytes 131096
  2.8 0.1 copy-done.1
  2.8 0.1 copy-done.2
  2.9 0.0 copy-done.4
  2.9 0.0 copy-done.3
  2.9 61.1 %shard_map.102 = (bf16[128,512]{1,0:T(8,128)(2,1)S(1)}, bf16[128,512]{1,0:T(8,128)(2,1)S(1)}, bf16[2,128,1024]{2,1,0:T(8,128)(2,1)S(1)}, bf16[2,256,512]{2,1,0:T(8,128)(2,1)S(1)}) custom-call(bf16[128,512]{1,0:T(8,128)(2,1)S(1)} %copy-done, bf16[128,512]{1,0:T(8,128)(2,1)S(1)} %copy-done.1, s32[2,128]{1,0:T(2,128)S(1)} %bitcast.14, f32[2,128]{1,0:T(2,128)S(1)} %bitcast.15, ...), custom_call_target="tpu_custom_call" | custom-call | tf_op jit(solution)/shard_map/pallas_call | solution.py:356
  64.0 1.3 %copy.13 = bf16[128,2,1024]{2,1,0:T(2,128)(2,1)} copy(bf16[128,2,1024]{2,0,1:T(8,128)(2,1)S(1)} %bitcast.13) | data formatting | bytes 1048576
  65.4 1.3 %copy.14 = bf16[256,2,512]{2,1,0:T(2,128)(2,1)} copy(bf16[256,2,512]{2,0,1:T(8,128)(2,1)S(1)} %bitcast.12) | data formatting | bytes 1048576
  66.7 0.7 copy.21
  67.4 0.7 copy.22
Async XLA Ops:
  0.6 1.2 %copy-start.5 = (bf16[256,2,512]{2,1,0:T(2,128)(2,1)S(1)}, bf16[256,2,512]{2,1,0:T(2,128)(2,1)}, u32[]{:S(2)}) copy-start(bf16[256,2,512]{2,1,0:T(2,128)(2,1)} %param.13) | copy-start | bytes 1572868
  1.9 0.9 %copy-start = (bf16[128,512]{1,0:T(8,128)(2,1)S(1)}, bf16[128,512]{1,0:T(8,128)(2,1)}, u32[]{:S(2)}) copy-start(bf16[128,512]{1,0:T(8,128)(2,1)} %states.1) | copy-start | bytes 393220
  1.9 1.0 %copy-start.1 = (bf16[128,512]{1,0:T(8,128)(2,1)S(1)}, bf16[128,512]{1,0:T(8,128)(2,1)}, u32[]{:S(2)}) copy-start(bf16[128,512]{1,0:T(8,128)(2,1)} %rates.1) | copy-start | bytes 393220
  1.9 1.0 %copy-start.2 = (bf16[128,512]{1,0:T(8,128)(2,1)S(1)}, bf16[128,512]{1,0:T(8,128)(2,1)}, u32[]{:S(2)}) copy-start(bf16[128,512]{1,0:T(8,128)(2,1)} %cotangent.1) | copy-start | bytes 393220
  1.9 1.0 %copy-start.4 = (f32[128,2]{0,1:T(2,128)S(1)}, f32[128,2]{0,1:T(2,128)}, u32[]{:S(2)}) copy-start(f32[128,2]{0,1:T(2,128)} %param.10) | copy-start | bytes 3076
  2.0 0.9 %copy-start.3 = (s32[128,2]{0,1:T(2,128)S(1)}, s32[128,2]{0,1:T(2,128)}, u32[]{:S(2)}) copy-start(s32[128,2]{0,1:T(2,128)} %param.9) | copy-start | bytes 3076

commit v4 on v3

--- a/solution.py
+++ b/solution.py
@@ -26,7 +26,7 @@
     tok_send, tok_recv, ret_send, ret_recv,
     full_in, full_out, part_in, part_out,
     first_in, first_out, sum_in, sum_out, second_in, second_out,
-    acc_v, acc_r, picks, knots_t,
+    hid, inn, picks, knots_t,
     tok_ss, tok_rs, ret_ss, ret_rs,
     w_ss, w_rs, one_ss, one_rs, two_ss, two_rs,
 ):
@@ -35,7 +35,6 @@
     hidden_all = w_in.shape[2]
     hrows = w_out.shape[1]
     slots = groups * local * cap
-    lines = local * groups * cap
     sets = nx // local
     g = lax.axis_index("expert")
     f = lax.axis_index("fsdp")
@@ -163,15 +162,57 @@
             shard_arrival(arr, i, 0).wait_recv()
             for j in range(1, ny):
                 along_y(arr, i, j).start()
-    over_peers(lambda d, o: tok_arrival(d, o).wait_recv())
     for arr in range(2):
         for j in range(1, ny):
             for i in range(nx):
                 shard_arrival(arr, i, j).wait_recv()
 
+    def ret_copy(d, o):
+        other, c = turn(g, o, groups), turn(mine, d, local)
+        return push(
+            ret_send.at[c, other], ret_recv.at[g, mine], ret_ss.at[c, other], ret_rs.at[g, mine],
+            expert=other, fsdp=y * nx + q * local + c,
+        )
+
+    def ret_arrival(d, o):
+        other, c = turn(g, o, groups), turn(mine, d, local)
+        return push(
+            ret_send.at[c, other], ret_recv.at[other, c], ret_ss.at[c, other], ret_rs.at[other, c],
+            expert=other, fsdp=y * nx + q * local + c,
+        )
+
     width = max(256, hrows)
     per = width // hrows
     steps = span // width
+    lines = groups * cap
+    for d in range(local):
+        column = turn(mine, d, local)
+        over_groups(0 if d else 1, lambda o: tok_arrival(d, o).wait_recv())
+
+        def rows_chunk(c, carry):
+            knots = tok_recv[column, :, 0].reshape(lines, feature)
+            grads = tok_recv[column, :, 1].reshape(lines, feature)
+            columns = pl.ds(pl.multiple_of(c * width, width), width)
+            wi = full_in[:, :, columns].reshape(feature, width)
+            wo = full_out[pl.ds(c * per, per)].reshape(width, feature)
+            preact = dot(knots, wi, 1, 0)
+            slope = dot(grads, wo, 1, 1)
+            sigma = jax.nn.sigmoid(preact)
+            hid[column, :, columns] = (preact * sigma).astype(BF)
+            inn[column, :, columns] = (
+                slope * (sigma * (1.0 + preact * (1.0 - sigma)))
+            ).astype(BF)
+            return carry
+
+        lax.fori_loop(0, hidden_all // width, rows_chunk, 0)
+        back = (groups, cap, feature)
+        wo = full_out[...].reshape(hidden_all, feature)
+        ret_send[column, :, 0] = dot(hid[column], wo, 1, 0).astype(BF).reshape(back)
+        wi = full_in[...].reshape(feature, hidden_all)
+        ret_send[column, :, 1] = dot(inn[column], wi, 1, 1).astype(BF).reshape(back)
+        over_groups(0 if d else 1, lambda o: ret_copy(d, o).start())
+        if d == 0:
+            ret_recv[g, mine] = ret_send[mine, g]
 
     def one_copy(arr, j, i, row):
         there, column = turn(y, j, ny), turn(x, i, nx)
@@ -205,35 +246,25 @@
             fsdp=there * nx + x,
         )
 
-    knots_t[...] = tok_recv[:, :, 0].reshape(lines, feature).T
-    acc_v[...] = jnp.zeros_like(acc_v)
-    acc_r[...] = jnp.zeros_like(acc_r)
+    knots_t[...] = tok_recv[:, :, 0].reshape(local * lines, feature).T
     for stage in range(1, ny + 1):
         row = turn(y, stage, ny)
 
-        def chunk(c, carry):
-            knots = tok_recv[:, :, 0].reshape(lines, feature)
-            grads = tok_recv[:, :, 1].reshape(lines, feature)
+        def grad_chunk(c, carry):
+            grads = tok_recv[:, :, 1].reshape(local * lines, feature)
             at = row * steps + c
             columns = pl.ds(pl.multiple_of(at * width, width), width)
-            wi = full_in[:, :, columns].reshape(feature, width)
-            wo = full_out[pl.ds(at * per, per)].reshape(width, feature)
-            preact = dot(knots, wi, 1, 0)
-            slope = dot(grads, wo, 1, 1)
-            sigma = jax.nn.sigmoid(preact)
-            hidden = (preact * sigma).astype(BF)
-            inner = (slope * (sigma * (1.0 + preact * (1.0 - sigma)))).astype(BF)
+            hidden = hid[:, :, columns].reshape(local * lines, width)
+            inner = inn[:, :, columns].reshape(local * lines, width)
+            part_out[pl.ds(at * per, per)] = dot(hidden, grads, 0, 0).astype(BF).reshape(
+                per, hrows, feature
+            )
             part_in[:, :, columns] = dot(knots_t[...], inner, 1, 0).astype(BF).reshape(
                 fsdp, feature // fsdp, width
             )
-            part_out[pl.ds(at * per, per)] = dot(hidden, grads, 0, 0).astype(BF).reshape(
-                per, hrows, feature
-            )
-            acc_v[...] += dot(hidden, wo, 1, 0)
-            acc_r[...] += dot(inner, wi, 1, 1)
             return carry
 
-        lax.fori_loop(0, steps, chunk, 0)
+        lax.fori_loop(0, steps, grad_chunk, 0)
         for i in range(1, nx):
             if stage < ny:
                 one_copy(1, stage, i, 0).start()
@@ -245,27 +276,6 @@
             one_copy(0, j, 0, turn(y, stage, ny)).start()
     for j in range(1, ny):
         one_copy(1, j, 0, 0).start()
-
-    back = (local, groups, cap, feature)
-    ret_send[:, :, 0] = acc_v[...].astype(BF).reshape(back)
-    ret_send[:, :, 1] = acc_r[...].astype(BF).reshape(back)
-
-    def ret_copy(d, o):
-        other, c = turn(g, o, groups), turn(mine, d, local)
-        return push(
-            ret_send.at[c, other], ret_recv.at[g, mine], ret_ss.at[c, other], ret_rs.at[g, mine],
-            expert=other, fsdp=y * nx + q * local + c,
-        )
-
-    def ret_arrival(d, o):
-        other, c = turn(g, o, groups), turn(mine, d, local)
-        return push(
-            ret_send.at[c, other], ret_recv.at[other, c], ret_ss.at[c, other], ret_rs.at[other, c],
-            expert=other, fsdp=y * nx + q * local + c,
-        )
-
-    over_peers(lambda d, o: ret_copy(d, o).start(), -1)
-    ret_recv[g, mine] = ret_send[mine, g]
 
     def two_copy(arr, i):
         to = turn(x, i, nx)
@@ -378,8 +388,8 @@
             pltpu.VMEM((nx,) + shard_out, BF),
             pltpu.VMEM((nx,) + shard_in, BF),
             pltpu.VMEM((nx,) + shard_out, BF),
-            pltpu.VMEM((local * groups * cap, feature), F32),
-            pltpu.VMEM((local * groups * cap, feature), F32),
+            pltpu.VMEM((local, groups * cap, hidden), BF),
+            pltpu.VMEM((local, groups * cap, hidden), BF),
             pltpu.VMEM((2, slots, rows), BF),
             pltpu.VMEM((feature, local * groups * cap), BF),
             dma((groups, local)),

time: 68.2 us -> 70 us (1.026)
  Pallas kernels: 61.1 us -> 62.9 us
    pallas_call x1, Pallas kernels: 61.1 us -> 62.9 us  [on_device(): pl.pallas_call(functools.partial(kernel, (groups, fsdp, nx, ny, local, ca...]
where the time goes in v4:
time: 70 us; the launch traced here: 69.8 us
  Pallas kernels  62.9 us (90%)
  local copies, waits for them, and re-layouts  6.18 us (9%)
  between operations  0.71 us (1%)
    pallas_call x1, Pallas kernels, on_device(): pl.pallas_call(functools.partial(kernel, (groups, fsdp, nx, ny, local, ca...  62.9 us
    unnamed x18, local copies, waits for them, and re-layouts  6.18 us

profile of v4, /device:TPU:0, one launch (start us, length us, event | category | flops | bytes accessed | tf_op | source)
XLA Modules:
  0.0 69.8 jit_solution(6063554800298420391)
XLA Ops:
  0.6 0.0 copy-start.5
  0.6 1.2 %copy.18 = bf16[128,2,1024]{2,0,1:T(8,128)(2,1)S(1)} copy(bf16[128,2,1024]{2,1,0:T(2,128)(2,1)} %param.12) | data formatting | bytes 1048576 | tf_op args[5]
  1.9 0.0 copy-done.5
  1.9 0.0 copy-start
  1.9 0.0 copy-start.1
  1.9 0.0 copy-start.2
  1.9 0.0 copy-start.4
  1.9 0.1 copy.17
  2.0 0.0 copy-start.3
  2.0 0.8 %copy-done = bf16[128,512]{1,0:T(8,128)(2,1)S(1)} copy-done((bf16[128,512]{1,0:T(8,128)(2,1)S(1)}, bf16[128,512]{1,0:T(8,128)(2,1)}, u32[]{:S(2)}) %copy-start) | copy-done | bytes 131096
  2.8 0.1 copy-done.1
  2.8 0.1 copy-done.2
  2.9 0.0 copy-done.4
  2.9 0.0 copy-done.3
  2.9 62.9 %shard_map.102 = (bf16[128,512]{1,0:T(8,128)(2,1)S(1)}, bf16[128,512]{1,0:T(8,128)(2,1)S(1)}, bf16[2,128,1024]{2,1,0:T(8,128)(2,1)S(1)}, bf16[2,256,512]{2,1,0:T(8,128)(2,1)S(1)}) custom-call(bf16[128,512]{1,0:T(8,128)(2,1)S(1)} %copy-done, bf16[128,512]{1,0:T(8,128)(2,1)S(1)} %copy-done.1, s32[2,128]{1,0:T(2,128)S(1)} %bitcast.14, f32[2,128]{1,0:T(2,128)S(1)} %bitcast.15, ...), custom_call_target="tpu_custom_call" | custom-call | tf_op jit(solution)/shard_map/pallas_call | solution.py:366
  65.8 1.3 %copy.13 = bf16[128,2,1024]{2,1,0:T(2,128)(2,1)} copy(bf16[128,2,1024]{2,0,1:T(8,128)(2,1)S(1)} %bitcast.13) | data formatting | bytes 1048576
  67.2 1.3 %copy.14 = bf16[256,2,512]{2,1,0:T(2,128)(2,1)} copy(bf16[256,2,512]{2,0,1:T(8,128)(2,1)S(1)} %bitcast.12) | data formatting | bytes 1048576
  68.5 0.7 copy.21
  69.2 0.7 copy.22
Async XLA Ops:
  0.6 1.2 %copy-start.5 = (bf16[256,2,512]{2,1,0:T(2,128)(2,1)S(1)}, bf16[256,2,512]{2,1,0:T(2,128)(2,1)}, u32[]{:S(2)}) copy-start(bf16[256,2,512]{2,1,0:T(2,128)(2,1)} %param.13) | copy-start | bytes 1572868
  1.9 0.9 %copy-start = (bf16[128,512]{1,0:T(8,128)(2,1)S(1)}, bf16[128,512]{1,0:T(8,128)(2,1)}, u32[]{:S(2)}) copy-start(bf16[128,512]{1,0:T(8,128)(2,1)} %states.1) | copy-start | bytes 393220
  1.9 1.0 %copy-start.1 = (bf16[128,512]{1,0:T(8,128)(2,1)S(1)}, bf16[128,512]{1,0:T(8,128)(2,1)}, u32[]{:S(2)}) copy-start(bf16[128,512]{1,0:T(8,128)(2,1)} %rates.1) | copy-start | bytes 393220
  1.9 1.0 %copy-start.2 = (bf16[128,512]{1,0:T(8,128)(2,1)S(1)}, bf16[128,512]{1,0:T(8,128)(2,1)}, u32[]{:S(2)}) copy-start(bf16[128,512]{1,0:T(8,128)(2,1)} %cotangent.1) | copy-start | bytes 393220
  1.9 1.0 %copy-start.4 = (f32[128,2]{0,1:T(2,128)S(1)}, f32[128,2]{0,1:T(2,128)}, u32[]{:S(2)}) copy-start(f32[128,2]{0,1:T(2,128)} %param.10) | copy-start | bytes 3076
  2.0 0.9 %copy-start.3 = (s32[128,2]{0,1:T(2,128)S(1)}, s32[128,2]{0,1:T(2,128)}, u32[]{:S(2)}) copy-start(s32[128,2]{0,1:T(2,128)} %param.9) | copy-start | bytes 3076

commit v5 on v3

--- a/solution.py
+++ b/solution.py
@@ -85,27 +85,55 @@
             greet(fsdp=y * nx + turn(q, k, sets) * local + d)
     for j in range(1, ny):
         greet(fsdp=turn(y, j, ny) * nx + x)
-    def along_x(arr, i):
+    def span_at(k):
+        return pl.ds(pl.multiple_of(turn(y, k, ny) * span, span), span)
+
+    def along_x(arr, i, k):
         to = turn(x, i, nx)
-        return push(
-            shards[arr].at[lax.rem(to, local)], fulls[arr].at[f],
-            w_ss.at[arr, i - 1], w_rs.at[arr, f], fsdp=y * nx + to,
-        )
-
-    def along_y(arr, i, j):
+        src, dst = shards[arr].at[lax.rem(to, local)], fulls[arr].at[f]
+        if arr == 0:
+            src, dst = src.at[:, span_at(k)], dst.at[:, span_at(k)]
+        return push(
+            src, dst, w_ss.at[arr, i, 0, k], w_rs.at[arr, f, turn(y, k, ny) if arr == 0 else 0],
+            fsdp=y * nx + to,
+        )
+
+    def along_y(arr, i, j, k):
         source = y * nx + turn(x, i, nx)
         src = shards[arr].at[mine] if i == 0 else fulls[arr].at[source]
-        return push(
-            src, fulls[arr].at[source], w_ss.at[arr, nx - 1 + i * (ny - 1) + j - 1],
-            w_rs.at[arr, source], fsdp=turn(y, j, ny) * nx + x,
-        )
-
-    def shard_arrival(arr, i, j):
+        dst = fulls[arr].at[source]
+        if arr == 0:
+            src, dst = src.at[:, span_at(k)], dst.at[:, span_at(k)]
+        return push(
+            src, dst, w_ss.at[arr, i, j, k],
+            w_rs.at[arr, source, turn(y, k, ny) if arr == 0 else 0],
+            fsdp=turn(y, j, ny) * nx + x,
+        )
+
+    arrived = set()
+
+    def await_shard(arr, i, j, k):
+        if (i, j) == (0, 0) or (arr, i, j, k) in arrived:
+            return
+        arrived.add((arr, i, j, k))
         source = turn(y, j, ny) * nx + turn(x, i, nx)
-        return push(
-            fulls[arr].at[source], fulls[arr].at[source], w_ss.at[arr, 0], w_rs.at[arr, source],
+        piece = fulls[arr].at[source]
+        if arr == 0:
+            piece = piece.at[:, span_at(k)]
+        push(
+            piece, piece, w_ss.at[arr, 0, 0, 0],
+            w_rs.at[arr, source, turn(y, k, ny) if arr == 0 else 0],
             fsdp=turn(y, j, ny) * nx + (x if j else turn(x, i, nx)),
-        )
+        ).wait_recv()
+
+    def send_along_y(i, stage):
+        for j in range(1, ny):
+            if stage == ny - j:
+                await_shard(1, i, 0, 0)
+                along_y(1, i, j, 0).start()
+            k = (j + stage) % ny
+            await_shard(0, i, 0, k)
+            along_y(0, i, j, k).start()
 
     experts_all = groups * local
     id_f = ids[...].astype(F32)
@@ -148,26 +176,23 @@
 
     pl.semaphore_wait(barrier, groups * local - 1 + nx - local + ny - 1)
 
-    for arr in range(2):
+    for i in range(1, nx):
+        along_x(1, i, 0).start()
+    send_along_y(0, 1)
+    for k in range(ny):
         for i in range(1, nx):
-            along_x(arr, i).start()
-        for j in range(1, ny):
-            along_y(arr, 0, j).start()
+            along_x(0, i, k).start()
     over_peers(lambda d, o: tok_copy(d, o).start())
     tok_recv[mine, g] = tok_send[g, mine]
     for arr in range(2):
         fulls[arr][f] = shards[arr][mine]
 
-    for arr in range(2):
-        for i in range(1, nx):
-            shard_arrival(arr, i, 0).wait_recv()
-            for j in range(1, ny):
-                along_y(arr, i, j).start()
+    for i in range(1, nx):
+        send_along_y(i, 1)
+    for stage in range(2, ny + 1):
+        for i in range(nx):
+            send_along_y(i, stage)
     over_peers(lambda d, o: tok_arrival(d, o).wait_recv())
-    for arr in range(2):
-        for j in range(1, ny):
-            for i in range(nx):
-                shard_arrival(arr, i, j).wait_recv()
 
     width = max(256, hrows)
     per = width // hrows
@@ -210,6 +235,10 @@
     acc_r[...] = jnp.zeros_like(acc_r)
     for stage in range(1, ny + 1):
         row = turn(y, stage, ny)
+        for i in range(nx):
+            await_shard(1, i, stage % ny, 0)
+            for j in range(ny):
+                await_shard(0, i, j, stage % ny)
 
         def chunk(c, carry):
             knots = tok_recv[:, :, 0].reshape(lines, feature)
@@ -267,40 +296,48 @@
     over_peers(lambda d, o: ret_copy(d, o).start(), -1)
     ret_recv[g, mine] = ret_send[mine, g]
 
-    def two_copy(arr, i):
+    def two_copy(arr, i, k):
         to = turn(x, i, nx)
-        return push(
-            sums[arr].at[to], seconds[arr].at[x], two_ss.at[arr, to], two_rs.at[arr, x],
-            fsdp=y * nx + to,
+        src, dst = sums[arr].at[to], seconds[arr].at[x]
+        if arr == 0:
+            src, dst = src.at[:, span_at(k)], dst.at[:, span_at(k)]
+        return push(
+            src, dst, two_ss.at[arr, to, k], two_rs.at[arr, x, k], fsdp=y * nx + to,
         )
 
     def two_arrival(arr, source):
-        return push(
-            sums[arr].at[source], seconds[arr].at[source], two_ss.at[arr, source],
-            two_rs.at[arr, source], fsdp=y * nx + source,
-        )
-
-    def summed(arr, i):
+        for k in range(ny if arr == 0 else 1):
+            piece = seconds[arr].at[source]
+            if arr == 0:
+                piece = piece.at[:, span_at(k)]
+            push(
+                piece, piece, two_ss.at[arr, source, k], two_rs.at[arr, source, k],
+                fsdp=y * nx + source,
+            ).wait_recv()
+
+    def summed(arr, i, k):
         column = turn(x, i, nx)
-        total = parts[arr][y * nx + column].astype(F32)
+        place = span_at(k) if arr == 0 else slice(None)
+        total = parts[arr][y * nx + column, :, place].astype(F32)
         for j in range(1, ny):
-            for row in range(ny if arr == 0 else 1):
-                one_arrival(arr, j, i, row).wait_recv()
-            total = total + firsts[arr][turn(y, j, ny), column].astype(F32)
+            one_arrival(arr, j, i, turn(y, k, ny)).wait_recv()
+            total = total + firsts[arr][turn(y, j, ny), column, :, place].astype(F32)
         return total
 
-    for i in range(1, nx):
-        for arr in (1, 0):
-            sums[arr][turn(x, i, nx)] = summed(arr, i).astype(BF)
-            two_copy(arr, i).start()
-    own = [summed(arr, 0) for arr in range(2)]
-    for arr in range(2):
-        total = own[arr]
-        for k in range(1, sets):
-            source = turn(q, k, sets) * local + mine
-            two_arrival(arr, source).wait_recv()
-            total = total + seconds[arr][source].astype(F32)
-        outs[arr][mine] = total.astype(BF)
+    for arr, k in [(1, 0)] + [(0, k) for k in range(ny)]:
+        place = span_at(k) if arr == 0 else slice(None)
+        for i in range(1, nx):
+            sums[arr][turn(x, i, nx), :, place] = summed(arr, i, k).astype(BF)
+            two_copy(arr, i, k).start()
+    for arr, k in [(0, k) for k in range(ny)] + [(1, 0)]:
+        place = span_at(k) if arr == 0 else slice(None)
+        total = summed(arr, 0, k)
+        for other in range(1, sets):
+            source = turn(q, other, sets) * local + mine
+            if k == 0:
+                two_arrival(arr, source)
+            total = total + seconds[arr][source, :, place].astype(F32)
+        outs[arr][mine, :, place] = total.astype(BF)
 
     over_peers(lambda d, o: ret_arrival(d, o).wait_recv())
     values = ret_recv[:, :, 0].reshape(slots, feature)
@@ -318,7 +355,7 @@
             total = None
             for k in range(sets):
                 source = turn(q, k, sets) * local + e
-                two_arrival(arr, source).wait_recv()
+                two_arrival(arr, source)
                 term = seconds[arr][source].astype(F32)
                 total = term if total is None else total + term
             outs[arr][e] = total.astype(BF)
@@ -327,11 +364,13 @@
     over_peers(lambda d, o: ret_copy(d, o).wait_send())
     for arr in range(2):
         for i in range(1, nx):
-            along_x(arr, i).wait_send()
-            two_copy(arr, i).wait_send()
+            for k in range(ny if arr == 0 else 1):
+                along_x(arr, i, k).wait_send()
+                two_copy(arr, i, k).wait_send()
         for j in range(1, ny):
             for i in range(nx):
-                along_y(arr, i, j).wait_send()
+                for k in range(ny if arr == 0 else 1):
+                    along_y(arr, i, j, k).wait_send()
                 for row in range(ny if arr == 0 else 1):
                     one_copy(arr, j, i, row).wait_send()
 
@@ -386,12 +425,12 @@
             dma((local, groups)),
             dma((local, groups)),
             dma((groups, local)),
-            dma((2, fsdp + nx)),
-            dma((2, fsdp)),
+            dma((2, nx, ny, ny)),
+            dma((2, fsdp, ny)),
             dma((2, ny, nx, ny)),
             dma((2, ny, nx, ny)),
-            dma((2, nx)),
-            dma((2, nx)),
+            dma((2, nx, ny)),
+            dma((2, nx, ny)),
         ],
         compiler_params=pltpu.CompilerParams(
             collective_id=0, has_side_effects=True, vmem_limit_bytes=36 * 1024 * 1024

time: 68.2 us -> 68 us (level)
  no operation moved by 1% of the time
where the time goes in v5:
time: 68 us; the launch traced here: 67.9 us
  Pallas kernels  61 us (90%)
  local copies, waits for them, and re-layouts  6.18 us (9%)
  between operations  0.71 us (1%)
    pallas_call x1, Pallas kernels, on_device(): pl.pallas_call(functools.partial(kernel, (groups, fsdp, nx, ny, local, ca...  61 us
    unnamed x18, local copies, waits for them, and re-layouts  6.18 us

profile of v5, /device:TPU:0, one launch (start us, length us, event | category | flops | bytes accessed | tf_op | source)
XLA Modules:
  0.0 67.9 jit_solution(15213324728885393274)
XLA Ops:
  0.6 0.0 copy-start.5
  0.6 1.2 %copy.18 = bf16[128,2,1024]{2,0,1:T(8,128)(2,1)S(1)} copy(bf16[128,2,1024]{2,1,0:T(2,128)(2,1)} %param.12) | data formatting | bytes 1048576 | tf_op args[5]
  1.9 0.0 copy-done.5
  1.9 0.0 copy-start
  1.9 0.0 copy-start.1
  1.9 0.0 copy-start.2
  1.9 0.0 copy-start.4
  1.9 0.1 copy.17
  2.0 0.0 copy-start.3
  2.0 0.8 %copy-done = bf16[128,512]{1,0:T(8,128)(2,1)S(1)} copy-done((bf16[128,512]{1,0:T(8,128)(2,1)S(1)}, bf16[128,512]{1,0:T(8,128)(2,1)}, u32[]{:S(2)}) %copy-start) | copy-done | bytes 131096
  2.8 0.1 copy-done.1
  2.8 0.1 copy-done.2
  2.9 0.0 copy-done.4
  2.9 0.0 copy-done.3
  2.9 61.0 %shard_map.102 = (bf16[128,512]{1,0:T(8,128)(2,1)S(1)}, bf16[128,512]{1,0:T(8,128)(2,1)S(1)}, bf16[2,128,1024]{2,1,0:T(8,128)(2,1)S(1)}, bf16[2,256,512]{2,1,0:T(8,128)(2,1)S(1)}) custom-call(bf16[128,512]{1,0:T(8,128)(2,1)S(1)} %copy-done, bf16[128,512]{1,0:T(8,128)(2,1)S(1)} %copy-done.1, s32[2,128]{1,0:T(2,128)S(1)} %bitcast.14, f32[2,128]{1,0:T(2,128)S(1)} %bitcast.15, ...), custom_call_target="tpu_custom_call" | custom-call | tf_op jit(solution)/shard_map/pallas_call | solution.py:395
  63.9 1.3 %copy.13 = bf16[128,2,1024]{2,1,0:T(2,128)(2,1)} copy(bf16[128,2,1024]{2,0,1:T(8,128)(2,1)S(1)} %bitcast.13) | data formatting | bytes 1048576
  65.2 1.3 %copy.14 = bf16[256,2,512]{2,1,0:T(2,128)(2,1)} copy(bf16[256,2,512]{2,0,1:T(8,128)(2,1)S(1)} %bitcast.12) | data formatting | bytes 1048576
  66.6 0.7 copy.21
  67.2 0.7 copy.22
Async XLA Ops:
  0.6 1.2 %copy-start.5 = (bf16[256,2,512]{2,1,0:T(2,128)(2,1)S(1)}, bf16[256,2,512]{2,1,0:T(2,128)(2,1)}, u32[]{:S(2)}) copy-start(bf16[256,2,512]{2,1,0:T(2,128)(2,1)} %param.13) | copy-start | bytes 1572868
  1.9 0.9 %copy-start = (bf16[128,512]{1,0:T(8,128)(2,1)S(1)}, bf16[128,512]{1,0:T(8,128)(2,1)}, u32[]{:S(2)}) copy-start(bf16[128,512]{1,0:T(8,128)(2,1)} %states.1) | copy-start | bytes 393220
  1.9 1.0 %copy-start.1 = (bf16[128,512]{1,0:T(8,128)(2,1)S(1)}, bf16[128,512]{1,0:T(8,128)(2,1)}, u32[]{:S(2)}) copy-start(bf16[128,512]{1,0:T(8,128)(2,1)} %rates.1) | copy-start | bytes 393220
  1.9 1.0 %copy-start.2 = (bf16[128,512]{1,0:T(8,128)(2,1)S(1)}, bf16[128,512]{1,0:T(8,128)(2,1)}, u32[]{:S(2)}) copy-start(bf16[128,512]{1,0:T(8,128)(2,1)} %cotangent.1) | copy-start | bytes 393220
  1.9 1.0 %copy-start.4 = (f32[128,2]{0,1:T(2,128)S(1)}, f32[128,2]{0,1:T(2,128)}, u32[]{:S(2)}) copy-start(f32[128,2]{0,1:T(2,128)} %param.10) | copy-start | bytes 3076
  2.0 0.9 %copy-start.3 = (s32[128,2]{0,1:T(2,128)S(1)}, s32[128,2]{0,1:T(2,128)}, u32[]{:S(2)}) copy-start(s32[128,2]{0,1:T(2,128)} %param.9) | copy-start | bytes 3076

commit v6 on v5

--- a/solution.py
+++ b/solution.py
@@ -26,7 +26,7 @@
     tok_send, tok_recv, ret_send, ret_recv,
     full_in, full_out, part_in, part_out,
     first_in, first_out, sum_in, sum_out, second_in, second_out,
-    acc_v, acc_r, picks, knots_t,
+    hid, inn, acc_v, acc_r, picks, knots_t,
     tok_ss, tok_rs, ret_ss, ret_rs,
     w_ss, w_rs, one_ss, one_rs, two_ss, two_rs,
 ):
@@ -35,7 +35,6 @@
     hidden_all = w_in.shape[2]
     hrows = w_out.shape[1]
     slots = groups * local * cap
-    lines = local * groups * cap
     sets = nx // local
     g = lax.axis_index("expert")
     f = lax.axis_index("fsdp")
@@ -192,11 +191,25 @@
     for stage in range(2, ny + 1):
         for i in range(nx):
             send_along_y(i, stage)
-    over_peers(lambda d, o: tok_arrival(d, o).wait_recv())
 
     width = max(256, hrows)
     per = width // hrows
     steps = span // width
+    lines = groups * cap
+
+    def ret_copy(d, o):
+        other, c = turn(g, o, groups), turn(mine, d, local)
+        return push(
+            ret_send.at[c, other], ret_recv.at[g, mine], ret_ss.at[c, other], ret_rs.at[g, mine],
+            expert=other, fsdp=y * nx + q * local + c,
+        )
+
+    def ret_arrival(d, o):
+        other, c = turn(g, o, groups), turn(mine, d, local)
+        return push(
+            ret_send.at[c, other], ret_recv.at[other, c], ret_ss.at[c, other], ret_rs.at[other, c],
+            expert=other, fsdp=y * nx + q * local + c,
+        )
 
     def one_copy(arr, j, i, row):
         there, column = turn(y, j, ny), turn(x, i, nx)
@@ -230,19 +243,13 @@
             fsdp=there * nx + x,
         )
 
-    knots_t[...] = tok_recv[:, :, 0].reshape(lines, feature).T
     acc_v[...] = jnp.zeros_like(acc_v)
     acc_r[...] = jnp.zeros_like(acc_r)
-    for stage in range(1, ny + 1):
-        row = turn(y, stage, ny)
-        for i in range(nx):
-            await_shard(1, i, stage % ny, 0)
-            for j in range(ny):
-                await_shard(0, i, j, stage % ny)
-
+
+    def rows_of(column, row):
         def chunk(c, carry):
-            knots = tok_recv[:, :, 0].reshape(lines, feature)
-            grads = tok_recv[:, :, 1].reshape(lines, feature)
+            knots = tok_recv[column, :, 0].reshape(lines, feature)
+            grads = tok_recv[column, :, 1].reshape(lines, feature)
             at = row * steps + c
             columns = pl.ds(pl.multiple_of(at * width, width), width)
             wi = full_in[:, :, columns].reshape(feature, width)
@@ -252,49 +259,64 @@
             sigma = jax.nn.sigmoid(preact)
             hidden = (preact * sigma).astype(BF)
             inner = (slope * (sigma * (1.0 + preact * (1.0 - sigma)))).astype(BF)
+            hid[column, :, columns] = hidden
+            inn[column, :, columns] = inner
+            acc_v[column] += dot(hidden, wo, 1, 0)
+            acc_r[column] += dot(inner, wi, 1, 1)
+            return carry
+
+        lax.fori_loop(0, steps, chunk, 0)
+
+    def grads_of(row):
+        def chunk(c, carry):
+            grads = tok_recv[:, :, 1].reshape(local * lines, feature)
+            at = row * steps + c
+            columns = pl.ds(pl.multiple_of(at * width, width), width)
+            hidden = hid[:, :, columns].reshape(local * lines, width)
+            inner = inn[:, :, columns].reshape(local * lines, width)
+            part_out[pl.ds(at * per, per)] = dot(hidden, grads, 0, 0).astype(BF).reshape(
+                per, hrows, feature
+            )
             part_in[:, :, columns] = dot(knots_t[...], inner, 1, 0).astype(BF).reshape(
                 fsdp, feature // fsdp, width
             )
-            part_out[pl.ds(at * per, per)] = dot(hidden, grads, 0, 0).astype(BF).reshape(
-                per, hrows, feature
-            )
-            acc_v[...] += dot(hidden, wo, 1, 0)
-            acc_r[...] += dot(inner, wi, 1, 1)
             return carry
 
         lax.fori_loop(0, steps, chunk, 0)
-        for i in range(1, nx):
-            if stage < ny:
-                one_copy(1, stage, i, 0).start()
-            for j in range(1, ny):
-                one_copy(0, j, i, row).start()
+
+    for d in range(local):
+        column = turn(mine, d, local)
+        over_groups(0 if d else 1, lambda o: tok_arrival(d, o).wait_recv())
+        knots_t[:, pl.ds(pl.multiple_of(column * lines, lines), lines)] = (
+            tok_recv[column, :, 0].reshape(lines, feature).T
+        )
+        for stage in range(1, ny + 1):
+            row = turn(y, stage, ny)
+            for i in range(nx):
+                await_shard(1, i, stage % ny, 0)
+                for j in range(ny):
+                    await_shard(0, i, j, stage % ny)
+            rows_of(column, row)
+            if stage == ny:
+                back = (groups, cap, feature)
+                ret_send[column, :, 0] = acc_v[column].astype(BF).reshape(back)
+                ret_send[column, :, 1] = acc_r[column].astype(BF).reshape(back)
+                over_groups(0 if d else 1, lambda o: ret_copy(d, o).start())
+                if d == 0:
+                    ret_recv[g, mine] = ret_send[mine, g]
+            if d == local - 1:
+                grads_of(row)
+                for i in range(1, nx):
+                    if stage < ny:
+                        one_copy(1, stage, i, 0).start()
+                    for j in range(1, ny):
+                        one_copy(0, j, i, row).start()
 
     for stage in range(1, ny + 1):
         for j in range(1, ny):
             one_copy(0, j, 0, turn(y, stage, ny)).start()
     for j in range(1, ny):
         one_copy(1, j, 0, 0).start()
-
-    back = (local, groups, cap, feature)
-    ret_send[:, :, 0] = acc_v[...].astype(BF).reshape(back)
-    ret_send[:, :, 1] = acc_r[...].astype(BF).reshape(back)
-
-    def ret_copy(d, o):
-        other, c = turn(g, o, groups), turn(mine, d, local)
-        return push(
-            ret_send.at[c, other], ret_recv.at[g, mine], ret_ss.at[c, other], ret_rs.at[g, mine],
-            expert=other, fsdp=y * nx + q * local + c,
-        )
-
-    def ret_arrival(d, o):
-        other, c = turn(g, o, groups), turn(mine, d, local)
-        return push(
-            ret_send.at[c, other], ret_recv.at[other, c], ret_ss.at[c, other], ret_rs.at[other, c],
-            expert=other, fsdp=y * nx + q * local + c,
-        )
-
-    over_peers(lambda d, o: ret_copy(d, o).start(), -1)
-    ret_recv[g, mine] = ret_send[mine, g]
 
     def two_copy(arr, i, k):
         to = turn(x, i, nx)
@@ -417,8 +439,10 @@
             pltpu.VMEM((nx,) + shard_out, BF),
             pltpu.VMEM((nx,) + shard_in, BF),
             pltpu.VMEM((nx,) + shard_out, BF),
-            pltpu.VMEM((local * groups * cap, feature), F32),
-            pltpu.VMEM((local * groups * cap, feature), F32),
+            pltpu.VMEM((local, groups * cap, hidden), BF),
+            pltpu.VMEM((local, groups * cap, hidden), BF),
+            pltpu.VMEM((local, groups * cap, feature), F32),
+            pltpu.VMEM((local, groups * cap, feature), F32),
             pltpu.VMEM((2, slots, rows), BF),
             pltpu.VMEM((feature, local * groups * cap), BF),
             dma((groups, local)),

time: 68 us -> 69.8 us (1.026)
  Pallas kernels: 61 us -> 62.8 us
    pallas_call x1, Pallas kernels: 61 us -> 62.8 us  [on_device(): pl.pallas_call(functools.partial(kernel, (groups, fsdp, nx, ny, local, ca...]
where the time goes in v6:
time: 69.8 us; the launch traced here: 69.7 us
  Pallas kernels  62.8 us (90%)
  local copies, waits for them, and re-layouts  6.18 us (9%)
  between operations  0.71 us (1%)
    pallas_call x1, Pallas kernels, on_device(): pl.pallas_call(functools.partial(kernel, (groups, fsdp, nx, ny, local, ca...  62.8 us
    unnamed x18, local copies, waits for them, and re-layouts  6.18 us

profile of v6, /device:TPU:0, one launch (start us, length us, event | category | flops | bytes accessed | tf_op | source)
XLA Modules:
  0.0 69.7 jit_solution(12668861430670320737)
XLA Ops:
  0.6 0.0 copy-start.5
  0.6 1.2 %copy.18 = bf16[128,2,1024]{2,0,1:T(8,128)(2,1)S(1)} copy(bf16[128,2,1024]{2,1,0:T(2,128)(2,1)} %param.12) | data formatting | bytes 1048576 | tf_op args[5]
  1.9 0.0 copy-done.5
  1.9 0.0 copy-start
  1.9 0.0 copy-start.1
  1.9 0.0 copy-start.2
  1.9 0.0 copy-start.4
  1.9 0.1 copy.17
  2.0 0.0 copy-start.3
  2.0 0.8 %copy-done = bf16[128,512]{1,0:T(8,128)(2,1)S(1)} copy-done((bf16[128,512]{1,0:T(8,128)(2,1)S(1)}, bf16[128,512]{1,0:T(8,128)(2,1)}, u32[]{:S(2)}) %copy-start) | copy-done | bytes 131096
  2.8 0.1 copy-done.1
  2.8 0.1 copy-done.2
  2.9 0.0 copy-done.4
  2.9 0.0 copy-done.3
  2.9 62.8 %shard_map.102 = (bf16[128,512]{1,0:T(8,128)(2,1)S(1)}, bf16[128,512]{1,0:T(8,128)(2,1)S(1)}, bf16[2,128,1024]{2,1,0:T(8,128)(2,1)S(1)}, bf16[2,256,512]{2,1,0:T(8,128)(2,1)S(1)}) custom-call(bf16[128,512]{1,0:T(8,128)(2,1)S(1)} %copy-done, bf16[128,512]{1,0:T(8,128)(2,1)S(1)} %copy-done.1, s32[2,128]{1,0:T(2,128)S(1)} %bitcast.14, f32[2,128]{1,0:T(2,128)S(1)} %bitcast.15, ...), custom_call_target="tpu_custom_call" | custom-call | tf_op jit(solution)/shard_map/pallas_call | solution.py:417
  65.7 1.3 %copy.13 = bf16[128,2,1024]{2,1,0:T(2,128)(2,1)} copy(bf16[128,2,1024]{2,0,1:T(8,128)(2,1)S(1)} %bitcast.13) | data formatting | bytes 1048576
  67.0 1.3 %copy.14 = bf16[256,2,512]{2,1,0:T(2,128)(2,1)} copy(bf16[256,2,512]{2,0,1:T(8,128)(2,1)S(1)} %bitcast.12) | data formatting | bytes 1048576
  68.4 0.7 copy.21
  69.0 0.7 copy.22
Async XLA Ops:
  0.6 1.2 %copy-start.5 = (bf16[256,2,512]{2,1,0:T(2,128)(2,1)S(1)}, bf16[256,2,512]{2,1,0:T(2,128)(2,1)}, u32[]{:S(2)}) copy-start(bf16[256,2,512]{2,1,0:T(2,128)(2,1)} %param.13) | copy-start | bytes 1572868
  1.9 0.9 %copy-start = (bf16[128,512]{1,0:T(8,128)(2,1)S(1)}, bf16[128,512]{1,0:T(8,128)(2,1)}, u32[]{:S(2)}) copy-start(bf16[128,512]{1,0:T(8,128)(2,1)} %states.1) | copy-start | bytes 393220
  1.9 1.0 %copy-start.1 = (bf16[128,512]{1,0:T(8,128)(2,1)S(1)}, bf16[128,512]{1,0:T(8,128)(2,1)}, u32[]{:S(2)}) copy-start(bf16[128,512]{1,0:T(8,128)(2,1)} %rates.1) | copy-start | bytes 393220
  1.9 1.0 %copy-start.2 = (bf16[128,512]{1,0:T(8,128)(2,1)S(1)}, bf16[128,512]{1,0:T(8,128)(2,1)}, u32[]{:S(2)}) copy-start(bf16[128,512]{1,0:T(8,128)(2,1)} %cotangent.1) | copy-start | bytes 393220
  1.9 1.0 %copy-start.4 = (f32[128,2]{0,1:T(2,128)S(1)}, f32[128,2]{0,1:T(2,128)}, u32[]{:S(2)}) copy-start(f32[128,2]{0,1:T(2,128)} %param.10) | copy-start | bytes 3076
  2.0 0.9 %copy-start.3 = (s32[128,2]{0,1:T(2,128)S(1)}, s32[128,2]{0,1:T(2,128)}, u32[]{:S(2)}) copy-start(s32[128,2]{0,1:T(2,128)} %param.9) | copy-start | bytes 3076

commit v7 on v6

--- a/solution.py
+++ b/solution.py
@@ -175,19 +175,22 @@
 
     pl.semaphore_wait(barrier, groups * local - 1 + nx - local + ny - 1)
 
+    over_groups(1, lambda o: tok_copy(0, o).start())
     for i in range(1, nx):
         along_x(1, i, 0).start()
     send_along_y(0, 1)
     for k in range(ny):
         for i in range(1, nx):
             along_x(0, i, k).start()
-    over_peers(lambda d, o: tok_copy(d, o).start())
     tok_recv[mine, g] = tok_send[g, mine]
     for arr in range(2):
         fulls[arr][f] = shards[arr][mine]
 
     for i in range(1, nx):
         send_along_y(i, 1)
+    over_groups(1, lambda o: tok_copy(0, o).wait_send())
+    for d in range(1, local):
+        over_groups(0, lambda o: tok_copy(d, o).start())
     for stage in range(2, ny + 1):
         for i in range(nx):
             send_along_y(i, stage)
@@ -382,7 +385,8 @@
                 total = term if total is None else total + term
             outs[arr][e] = total.astype(BF)
 
-    over_peers(lambda d, o: tok_copy(d, o).wait_send())
+    for d in range(1, local):
+        over_groups(0, lambda o: tok_copy(d, o).wait_send())
     over_peers(lambda d, o: ret_copy(d, o).wait_send())
     for arr in range(2):
         for i in range(1, nx):

time: 69.8 us -> 69.1 us (0.990)
  Pallas kernels: 62.8 us -> 62.1 us
    pallas_call x1, Pallas kernels: 62.8 us -> 62.1 us  [on_device(): pl.pallas_call(functools.partial(kernel, (groups, fsdp, nx, ny, local, ca...]
where the time goes in v7:
time: 69.1 us; the launch traced here: 69 us
  Pallas kernels  62.1 us (90%)
  local copies, waits for them, and re-layouts  6.18 us (9%)
  between operations  0.71 us (1%)
    pallas_call x1, Pallas kernels, on_device(): pl.pallas_call(functools.partial(kernel, (groups, fsdp, nx, ny, local, ca...  62.1 us
    unnamed x18, local copies, waits for them, and re-layouts  6.18 us

profile of v7, /device:TPU:0, one launch (start us, length us, event | category | flops | bytes accessed | tf_op | source)
XLA Modules:
  0.0 69.0 jit_solution(6396890036563171356)
XLA Ops:
  0.6 0.0 copy-start.5
  0.6 1.2 %copy.18 = bf16[128,2,1024]{2,0,1:T(8,128)(2,1)S(1)} copy(bf16[128,2,1024]{2,1,0:T(2,128)(2,1)} %param.12) | data formatting | bytes 1048576 | tf_op args[5]
  1.9 0.0 copy-done.5
  1.9 0.0 copy-start
  1.9 0.0 copy-start.1
  1.9 0.0 copy-start.2
  1.9 0.0 copy-start.4
  1.9 0.1 copy.17
  2.0 0.0 copy-start.3
  2.0 0.8 %copy-done = bf16[128,512]{1,0:T(8,128)(2,1)S(1)} copy-done((bf16[128,512]{1,0:T(8,128)(2,1)S(1)}, bf16[128,512]{1,0:T(8,128)(2,1)}, u32[]{:S(2)}) %copy-start) | copy-done | bytes 131096
  2.8 0.1 copy-done.1
  2.8 0.1 copy-done.2
  2.9 0.0 copy-done.4
  2.9 0.0 copy-done.3
  2.9 62.1 %shard_map.102 = (bf16[128,512]{1,0:T(8,128)(2,1)S(1)}, bf16[128,512]{1,0:T(8,128)(2,1)S(1)}, bf16[2,128,1024]{2,1,0:T(8,128)(2,1)S(1)}, bf16[2,256,512]{2,1,0:T(8,128)(2,1)S(1)}) custom-call(bf16[128,512]{1,0:T(8,128)(2,1)S(1)} %copy-done, bf16[128,512]{1,0:T(8,128)(2,1)S(1)} %copy-done.1, s32[2,128]{1,0:T(2,128)S(1)} %bitcast.14, f32[2,128]{1,0:T(2,128)S(1)} %bitcast.15, ...), custom_call_target="tpu_custom_call" | custom-call | tf_op jit(solution)/shard_map/pallas_call | solution.py:421
  65.0 1.3 %copy.13 = bf16[128,2,1024]{2,1,0:T(2,128)(2,1)} copy(bf16[128,2,1024]{2,0,1:T(8,128)(2,1)S(1)} %bitcast.13) | data formatting | bytes 1048576
  66.3 1.3 %copy.14 = bf16[256,2,512]{2,1,0:T(2,128)(2,1)} copy(bf16[256,2,512]{2,0,1:T(8,128)(2,1)S(1)} %bitcast.12) | data formatting | bytes 1048576
  67.6 0.7 copy.21
  68.3 0.7 copy.22
Async XLA Ops:
  0.6 1.2 %copy-start.5 = (bf16[256,2,512]{2,1,0:T(2,128)(2,1)S(1)}, bf16[256,2,512]{2,1,0:T(2,128)(2,1)}, u32[]{:S(2)}) copy-start(bf16[256,2,512]{2,1,0:T(2,128)(2,1)} %param.13) | copy-start | bytes 1572868
  1.9 0.9 %copy-start = (bf16[128,512]{1,0:T(8,128)(2,1)S(1)}, bf16[128,512]{1,0:T(8,128)(2,1)}, u32[]{:S(2)}) copy-start(bf16[128,512]{1,0:T(8,128)(2,1)} %states.1) | copy-start | bytes 393220
  1.9 1.0 %copy-start.1 = (bf16[128,512]{1,0:T(8,128)(2,1)S(1)}, bf16[128,512]{1,0:T(8,128)(2,1)}, u32[]{:S(2)}) copy-start(bf16[128,512]{1,0:T(8,128)(2,1)} %rates.1) | copy-start | bytes 393220
  1.9 1.0 %copy-start.2 = (bf16[128,512]{1,0:T(8,128)(2,1)S(1)}, bf16[128,512]{1,0:T(8,128)(2,1)}, u32[]{:S(2)}) copy-start(bf16[128,512]{1,0:T(8,128)(2,1)} %cotangent.1) | copy-start | bytes 393220
  1.9 1.0 %copy-start.4 = (f32[128,2]{0,1:T(2,128)S(1)}, f32[128,2]{0,1:T(2,128)}, u32[]{:S(2)}) copy-start(f32[128,2]{0,1:T(2,128)} %param.10) | copy-start | bytes 3076
  2.0 0.9 %copy-start.3 = (s32[128,2]{0,1:T(2,128)S(1)}, s32[128,2]{0,1:T(2,128)}, u32[]{:S(2)}) copy-start(s32[128,2]{0,1:T(2,128)} %param.9) | copy-start | bytes 3076

commit v8 on v5

--- a/solution.py
+++ b/solution.py
@@ -176,13 +176,15 @@
 
     pl.semaphore_wait(barrier, groups * local - 1 + nx - local + ny - 1)
 
+    over_groups(1, lambda o: tok_copy(0, o).start())
     for i in range(1, nx):
         along_x(1, i, 0).start()
     send_along_y(0, 1)
     for k in range(ny):
         for i in range(1, nx):
             along_x(0, i, k).start()
-    over_peers(lambda d, o: tok_copy(d, o).start())
+    for d in range(1, local):
+        over_groups(0, lambda o: tok_copy(d, o).start())
     tok_recv[mine, g] = tok_send[g, mine]
     for arr in range(2):
         fulls[arr][f] = shards[arr][mine]

time: 68 us -> 68 us (level)
  no operation moved by 1% of the time
where the time goes in v8:
time: 68 us; the launch traced here: 67.9 us
  Pallas kernels  61 us (90%)
  local copies, waits for them, and re-layouts  6.18 us (9%)
  between operations  0.71 us (1%)
    pallas_call x1, Pallas kernels, on_device(): pl.pallas_call(functools.partial(kernel, (groups, fsdp, nx, ny, local, ca...  61 us
    unnamed x18, local copies, waits for them, and re-layouts  6.18 us

profile of v8, /device:TPU:0, one launch (start us, length us, event | category | flops | bytes accessed | tf_op | source)
XLA Modules:
  0.0 67.9 jit_solution(4797635009038264773)
XLA Ops:
  0.6 0.0 copy-start.5
  0.6 1.2 %copy.18 = bf16[128,2,1024]{2,0,1:T(8,128)(2,1)S(1)} copy(bf16[128,2,1024]{2,1,0:T(2,128)(2,1)} %param.12) | data formatting | bytes 1048576 | tf_op args[5]
  1.9 0.0 copy-done.5
  1.9 0.0 copy-start
  1.9 0.0 copy-start.1
  1.9 0.0 copy-start.2
  1.9 0.0 copy-start.4
  1.9 0.1 copy.17
  2.0 0.0 copy-start.3
  2.0 0.8 %copy-done = bf16[128,512]{1,0:T(8,128)(2,1)S(1)} copy-done((bf16[128,512]{1,0:T(8,128)(2,1)S(1)}, bf16[128,512]{1,0:T(8,128)(2,1)}, u32[]{:S(2)}) %copy-start) | copy-done | bytes 131096
  2.8 0.1 copy-done.1
  2.8 0.1 copy-done.2
  2.9 0.0 copy-done.4
  2.9 0.0 copy-done.3
  2.9 61.0 %shard_map.102 = (bf16[128,512]{1,0:T(8,128)(2,1)S(1)}, bf16[128,512]{1,0:T(8,128)(2,1)S(1)}, bf16[2,128,1024]{2,1,0:T(8,128)(2,1)S(1)}, bf16[2,256,512]{2,1,0:T(8,128)(2,1)S(1)}) custom-call(bf16[128,512]{1,0:T(8,128)(2,1)S(1)} %copy-done, bf16[128,512]{1,0:T(8,128)(2,1)S(1)} %copy-done.1, s32[2,128]{1,0:T(2,128)S(1)} %bitcast.14, f32[2,128]{1,0:T(2,128)S(1)} %bitcast.15, ...), custom_call_target="tpu_custom_call" | custom-call | tf_op jit(solution)/shard_map/pallas_call | solution.py:397
  63.9 1.3 %copy.13 = bf16[128,2,1024]{2,1,0:T(2,128)(2,1)} copy(bf16[128,2,1024]{2,0,1:T(8,128)(2,1)S(1)} %bitcast.13) | data formatting | bytes 1048576
  65.2 1.3 %copy.14 = bf16[256,2,512]{2,1,0:T(2,128)(2,1)} copy(bf16[256,2,512]{2,0,1:T(8,128)(2,1)S(1)} %bitcast.12) | data formatting | bytes 1048576
  66.6 0.7 copy.21
  67.2 0.7 copy.22
Async XLA Ops:
  0.6 1.2 %copy-start.5 = (bf16[256,2,512]{2,1,0:T(2,128)(2,1)S(1)}, bf16[256,2,512]{2,1,0:T(2,128)(2,1)}, u32[]{:S(2)}) copy-start(bf16[256,2,512]{2,1,0:T(2,128)(2,1)} %param.13) | copy-start | bytes 1572868
  1.9 0.9 %copy-start = (bf16[128,512]{1,0:T(8,128)(2,1)S(1)}, bf16[128,512]{1,0:T(8,128)(2,1)}, u32[]{:S(2)}) copy-start(bf16[128,512]{1,0:T(8,128)(2,1)} %states.1) | copy-start | bytes 393220
  1.9 1.0 %copy-start.1 = (bf16[128,512]{1,0:T(8,128)(2,1)S(1)}, bf16[128,512]{1,0:T(8,128)(2,1)}, u32[]{:S(2)}) copy-start(bf16[128,512]{1,0:T(8,128)(2,1)} %rates.1) | copy-start | bytes 393220
  1.9 1.0 %copy-start.2 = (bf16[128,512]{1,0:T(8,128)(2,1)S(1)}, bf16[128,512]{1,0:T(8,128)(2,1)}, u32[]{:S(2)}) copy-start(bf16[128,512]{1,0:T(8,128)(2,1)} %cotangent.1) | copy-start | bytes 393220
  1.9 1.0 %copy-start.4 = (f32[128,2]{0,1:T(2,128)S(1)}, f32[128,2]{0,1:T(2,128)}, u32[]{:S(2)}) copy-start(f32[128,2]{0,1:T(2,128)} %param.10) | copy-start | bytes 3076
  2.0 0.9 %copy-start.3 = (s32[128,2]{0,1:T(2,128)S(1)}, s32[128,2]{0,1:T(2,128)}, u32[]{:S(2)}) copy-start(s32[128,2]{0,1:T(2,128)} %param.9) | copy-start | bytes 3076
